TPU v7x, 256 devices: a whole 4x4x8 slice. The times are simulated.
256 devices in a mesh: occ: 8 (over x_hi, y), vir: 32 (over x_lo, z, core).
Axes of the slice: x: 4 (x_hi: 2, x_lo: 2; x = x_hi * 2 + x_lo), y: 4, z: 8, core: 2. Of those that a mesh axis runs over, the one named last changes fastest.
Arguments:
- t2: float32 [512, 24576], P('occ', 'vir'), may hold values from -6 to 6
- integral_tiles: float32 [8, 2048, 128, 128], P('occ', 'vir'), may hold values from -0.0546875 to 0.0546875
- contract_tile: int32 [8, 2048], P('occ', 'vir'), may hold values from 0 to 5
- slot_of_block: int32 [8, 2048], P('occ', 'vir'), may hold values from 0 to 31
- residual_list: int32 [32, 32], replicated, may hold values from 0 to 191, as said below
- owner_pos: int32 [192], replicated, may hold values from 0 to 191, as said below
Outputs:
- ladder_residual: float32 [512, 24576], P('occ', 'vir')
Inputs may be any that keep to these rules, and one draw needn't show every extreme that they name: `residual_list`: each row names 32 distinct tiles; their owners owner_pos // 6 are 16 distinct values, each owning exactly 2 of the row's tiles. `owner_pos`: A permutation of the 192 tiles.
All inputs are finite; a program needn't handle non-finite values.
Results may differ from a plain program's by a relative error of at most 0.0001.
Values sent between devices are 32-bit elements; how exact they have to be, the bound alone decides.
No kernel may reach another device: no remote copies, remote signals or barrier semaphores. Data moves between devices by JAX's collectives and lax.ppermute only.
A program may use at most 128 MiB of HBM per device.

v0:
```python
import jax
import jax.numpy as jnp
from jax import lax
from jax.sharding import PartitionSpec as P


def shards(t2, integral_tiles, contract_tile, slot_of_block, residual_list, owner_pos):
    rows_dev = t2.shape[0]
    tile_width = integral_tiles.shape[-1]
    tiles_dev = t2.shape[1] // tile_width
    slot_count = residual_list.shape[1]
    blocks = integral_tiles.shape[1]
    highest = lax.Precision.HIGHEST
    pick_tile = (
        contract_tile[0][:, None] == jnp.arange(tiles_dev, dtype=jnp.int32)[None, :]
    ).astype(jnp.float32)
    pick_slot = (
        slot_of_block[0][:, None] == jnp.arange(slot_count, dtype=jnp.int32)[None, :]
    ).astype(jnp.float32)
    pairing = (pick_tile[:, :, None] * pick_slot[:, None, :]).reshape(
        blocks, tiles_dev * slot_count
    )
    flat_tiles = integral_tiles[0].reshape(blocks, tile_width * tile_width)
    summed = jnp.dot(pairing.T, flat_tiles, precision=highest, preferred_element_type=jnp.float32)
    dense_map = summed.reshape(tiles_dev, slot_count, tile_width, tile_width).transpose(0, 2, 1, 3)
    dense_map = dense_map.reshape(tiles_dev * tile_width, slot_count * tile_width)
    gathered = lax.all_gather(t2, "occ", axis=0, tiled=True)
    partial_value = lax.psum_scatter(
        jnp.dot(gathered, dense_map, precision=highest, preferred_element_type=jnp.float32),
        "occ",
        scatter_dimension=0,
        tiled=True,
    )
    vir_index = lax.axis_index("vir")
    positions_all = owner_pos[residual_list]
    own_positions = lax.dynamic_index_in_dim(positions_all, vir_index, 0, keepdims=False)
    pieces = partial_value.reshape(rows_dev, slot_count, tile_width)
    tile_total = owner_pos.shape[0]
    placement = (own_positions[:, None] == jnp.arange(tile_total, dtype=jnp.int32)[None, :]).astype(
        jnp.float32
    )
    spread = jnp.einsum(
        "sp,rsc->rpc", placement, pieces, precision=highest, preferred_element_type=jnp.float32
    )
    result = lax.psum_scatter(
        spread.reshape(rows_dev, tile_total * tile_width), "vir", scatter_dimension=1, tiled=True
    )
    return result


def solution(mesh):
    in_specs = (
        P("occ", "vir"),
        P("occ", "vir", None, None),
        P("occ", "vir"),
        P("occ", "vir"),
        P(),
        P(),
    )
    out_specs = P("occ", "vir")
    return jax.shard_map(shards, mesh=mesh, in_specs=in_specs, out_specs=out_specs, check_vma=False)
```

profile of v0, /device:TPU:32, one launch (start us, length us, event | category | flops | bytes accessed | tf_op | source)
XLA Modules:
  0.0 377.1 jit_solution(13057980540698665844)
XLA Ops:
  6.5 0.0 copy-start
  6.5 0.0 all-gather.2.cloned.1.call-start
  6.5 0.7 all-gather.2.cloned.1.call-update
  7.3 0.0 reduce-scatter.7.cloned.1.call-start
  7.3 0.7 fusion.17
  8.0 0.7 fusion.16
  8.6 16.8 %fusion.6 = f32[6,32,128,128]{3,1,2,0:T(8,128)} fusion(f32[64,32]{0,1:T(8,128)S(1)} %fusion.16, f32[64,6]{0,1:T(8,128)S(1)} %fusion.17, f32[8,8,128,128]{3,2,1,0:T(8,128)} %bitcast.58), kind=kOutput, calls=%fused_computation.8 | convolution fusion | flops 2415931392 | bytes 16786944 | tf_op jit(solution)/shard_map/dot_general | solution.py:24
  25.5 41.7 %all-gather.2.cloned.1.call-done = f32[512,768]{1,0:T(8,128)} async-done(((f32[64,768]{1,0:T(8,128)}), f32[512,768]{1,0:T(8,128)}) %all-gather.2.cloned.1.call-update) | async-done | bytes 1572880 | tf_op jit(solution)/shard_map/all_gather | solution.py:27
  67.1 44.9 %fusion.3 = f32[512,4096]{0,1:T(8,128)} fusion(f32[512,768]{1,0:T(8,128)} %all-gather.2.cloned.1.call-done, f32[96,8,32,128]{3,2,1,0:T(8,128)} %bitcast.54), kind=kOutput, calls=%fused_computation.4 | convolution fusion | flops 19327352832 | bytes 22544384 | tf_op jit(solution)/shard_map/dot_general | solution.py:29
  112.1 8.9 %copy.13 = f32[512,4096]{1,0:T(8,128)} copy(f32[512,4096]{0,1:T(8,128)} %fusion.3) | data formatting | bytes 16777216
  121.0 0.0 copy-start.1
  121.0 0.0 reduce-scatter.7.cloned.1.call-update
  121.0 0.0 reduce-scatter.5.cloned.1.call-start
  121.1 0.6 copy-done.1
  121.7 0.1 reshape.69
  121.8 0.0 copy-done
  121.8 7.1 %gather_fusion = s32[1024]{0:T(1024)S(1)} fusion(s32[192]{0:T(256)S(1)} %copy-done, s32[1024]{0:T(1024)S(1)} %broadcast_clamp_fusion), kind=kCustom, calls=%fused_computation | custom fusion | bytes 12288 | tf_op jit(solution)/shard_map/gather | solution.py:35
  128.9 0.1 reshape.68
  129.0 110.2 %reduce-scatter.7.cloned.1.call-done = f32[64,4096]{1,0:T(8,128)} async-done(((f32[512,4096]{1,0:T(8,128)}), f32[64,4096]{1,0:T(8,128)}) %reduce-scatter.7.cloned.1.call-update) | async-done | bytes 1048592
  239.2 1.8 copy.14
  241.0 1.0 copy.11
  242.0 2.8 fusion.13
  244.7 6.2 %copy.33 = f32[8,8,192,128]{3,1,2,0:T(8,128)} copy(f32[8,8,192,128]{3,2,1,0:T(8,128)S(1)} %bitcast.56) | data formatting | bytes 12582912
  250.9 0.0 reduce-scatter.5.cloned.1.call-update
  251.0 119.6 %reduce-scatter.5.cloned.1.call-done = f32[64,768]{1,0:T(8,128)} async-done(((f32[64,24576]{1,0:T(8,128)}), f32[64,768]{1,0:T(8,128)}) %reduce-scatter.5.cloned.1.call-update) | async-done | bytes 196624 | tf_op jit(solution)/shard_map/reduce_scatter | solution.py:45
  (3 shorter events, 0.0 us)
Async XLA Ops:
  6.5 115.3 %copy-start = (s32[192]{0:T(256)S(1)}, s32[192]{0:T(256)}, u32[]{:S(2)}) copy-start(s32[192]{0:T(256)} %param.11) | copy-start | bytes 2308
  6.5 60.6 %all-gather.2.cloned.1.call-start = ((), (), s32[]{:S(2)}) async-start(), calls=%async_computation.2 | async-start | bytes 1769472 | tf_op jit(solution)/shard_map/all_gather | solution.py:27
  7.3 231.9 %reduce-scatter.7.cloned.1.call-start = ((), (), s32[]{:S(2)}) async-start(), calls=%async_computation.4 | async-start | bytes 9437184
  121.0 0.7 copy-start.1
  121.0 249.5 %reduce-scatter.5.cloned.1.call-start = ((), (), s32[]{:S(2)}) async-start(), calls=%async_computation.3 | async-start | bytes 6488064 | tf_op jit(solution)/shard_map/reduce_scatter | solution.py:45
Sparse Core Ops, SparseCore 0:
  9.9 57.1 all-gather.1
  121.1 117.9 reduce-scatter.6
  251.1 119.4 reduce-scatter.4
where the time goes:
time: 382 us; the launch traced here: 377 us
  waiting for transfers between devices  272 us (71%)
  matrix products  64.5 us (17%)
  local copies, waits for them, and re-layouts  25.8 us (7%)
  between operations  13.1 us (3%)
    reduce_scatter x1, waiting for transfers between devices, shards(): lax.psum_scatter(spread.reshape(rows_dev, tile_total * tile_width), 'vir'...  120 us
    unnamed x4, waiting for transfers between devices  111 us
    dot_general x1, matrix products, shards(): jnp.dot(gathered, dense_map, precision=highest, preferred_element_type=jn...  44.9 us
    all_gather x1, waiting for transfers between devices, shards(): gathered = lax.all_gather(t2, 'occ', axis=0, tiled=True)  41.7 us
    unnamed x7, local copies, waits for them, and re-layouts  17.6 us
    dot_general x1, matrix products, shards(): jnp.dot(pairing.T, flat_tiles, precision=highest, preferred_element_type=...  16.8 us
  transfers between devices with their start and end apart: 3, of which 3 were waited for; matrix products, arithmetic and copies ran while one was open for 7% of the time, Pallas kernels for 0%

commit v1 on v0

v1 whole, which is shorter than its diff:
```python
import functools

import jax
import jax.numpy as jnp
from jax import lax
from jax.experimental import pallas as pl
from jax.experimental.pallas import tpu as pltpu
from jax.sharding import PartitionSpec as P

N_Y = 4
N_XH = 2
N_Z = 8
N_XL = 2
ROWS_A = 40
PRODUCT_MIB = 62


def from_occ(v, dx, dy):
    perm = [
        (((a + dx) % N_XH) * N_Y + (b + dy) % N_Y, a * N_Y + b)
        for a in range(N_XH)
        for b in range(N_Y)
    ]
    return lax.ppermute(v, "occ", perm)


def from_vir(v, dx, dc):
    perm = [
        ((((a + dx) % N_XL) * N_Z + z) * 2 + (c + dc) % 2, (a * N_Z + z) * 2 + c)
        for a in range(N_XL)
        for z in range(N_Z)
        for c in range(2)
    ]
    return lax.ppermute(v, "vir", perm)


def smem():
    return pl.BlockSpec(memory_space=pltpu.SMEM)


def vmem():
    return pl.BlockSpec(memory_space=pltpu.VMEM)


def hbm():
    return pl.BlockSpec(memory_space=pltpu.HBM)


def call(kernel, out_shape, in_specs, out_specs, scratch, nbytes, flops=0, limit=8):
    return pl.pallas_call(
        kernel,
        out_shape=out_shape,
        in_specs=in_specs,
        out_specs=out_specs,
        scratch_shapes=scratch,
        compiler_params=pltpu.CompilerParams(vmem_limit_bytes=limit * 1024 * 1024),
        cost_estimate=pl.CostEstimate(flops=flops, bytes_accessed=nbytes, transcendentals=0),
    )


def product_kernel(n_pieces, moves, *refs):
    con_ref, slot_ref, blocks = refs[:3]
    pieces = refs[3 : 3 + n_pieces]
    b_ref, t_ref, x_ref, acc_ref, block_sems, in_sems, out_sems = refs[-7:]
    outs = refs[3 + n_pieces : -7]
    n_blocks, width, _ = b_ref.shape
    n_parts = block_sems.shape[0]
    part = n_blocks // n_parts
    tiles = x_ref.shape[0]
    loads = []
    rows = pieces[0].shape[0]
    for i, piece in enumerate(pieces):
        load = pltpu.make_async_copy(piece, t_ref.at[pl.ds(i * rows, rows)], in_sems.at[i])
        load.start()
        loads.append(load)
    block_loads = []
    for i in range(n_parts):
        some = pl.ds(i * part, part)
        load = pltpu.make_async_copy(blocks.at[some], b_ref.at[some], block_sems.at[i])
        load.start()
        block_loads.append(load)
    acc_ref[...] = jnp.zeros_like(acc_ref)
    for i, load in enumerate(loads):
        load.wait()
        here = slice(i * rows, (i + 1) * rows)
        for c in range(tiles):
            a = t_ref[here, c * width : (c + 1) * width]
            high = a.astype(jnp.bfloat16)
            x_ref[c, here, :width] = high
            x_ref[c, here, width:] = (a - high.astype(jnp.float32)).astype(jnp.bfloat16)
    step = 4

    def body(k, carry):
        results = []
        for u in range(step):
            b = b_ref[k * step + u]
            high = b.astype(jnp.bfloat16)
            low = (b - high.astype(jnp.float32)).astype(jnp.bfloat16)
            w = jnp.concatenate([high, low], axis=1)
            w = jnp.concatenate([w, w], axis=0)
            x = x_ref[con_ref[0, k * step + u]]
            p = jnp.dot(x, w, preferred_element_type=jnp.float32)
            results.append(p[:, :width] + p[:, width:])
        for u in range(step):
            s = slot_ref[0, k * step + u]
            acc_ref[s] = acc_ref[s] + results[u]
        return carry

    for i, load in enumerate(block_loads):
        load.wait()
        lax.fori_loop(i * part // step, (i + 1) * part // step, body, 0)
    stores = []
    for n, (o, index, slot, slots, row, n_rows) in enumerate(moves):
        source = acc_ref.at[pl.ds(slot, slots), pl.ds(row, n_rows)]
        target = outs[o] if index is None else outs[o].at[index]
        store = pltpu.make_async_copy(source, target, out_sems.at[n])
        store.start()
        stores.append(store)
    for store in stores:
        store.wait()


def products(con, slot, blocks, pieces, slots, shapes, moves):
    n_blocks, width, _ = blocks.shape
    tiles = pieces[0].shape[1] // width
    n_rows = pieces[0].shape[0] * len(pieces)
    shapes = [jax.ShapeDtypeStruct(s, jnp.float32) for s in shapes]
    return call(
        functools.partial(product_kernel, len(pieces), moves),
        shapes,
        [smem(), smem()] + [hbm()] * (1 + len(pieces)),
        [hbm()] * len(shapes),
        [
            pltpu.VMEM(blocks.shape, jnp.float32),
            pltpu.VMEM((n_rows, tiles * width), jnp.float32),
            pltpu.VMEM((tiles, n_rows, 2 * width), jnp.bfloat16),
            pltpu.VMEM((slots, n_rows, width), jnp.float32),
            pltpu.SemaphoreType.DMA((4,)),
            pltpu.SemaphoreType.DMA((len(pieces),)),
            pltpu.SemaphoreType.DMA((len(moves),)),
        ],
        4 * (blocks.size + n_rows * (tiles + slots) * width),
        8 * n_blocks * n_rows * width * width,
        PRODUCT_MIB,
    )(con, slot, blocks, *pieces)


def sum_kernel(own, left_a, left_b, right_a, right_b, keep, give):
    half = left_a.shape[1]
    for out, d in ((give, 1), (keep, 0)):
        out[:half] = own[d, :half] + left_a[d] + right_a[d]
        out[half:] = own[d, half:] + left_b[d] + right_b[d]


def y_sum(own, left_a, left_b, right_a, right_b):
    shape = jax.ShapeDtypeStruct(own.shape[1:], jnp.float32)
    return call(sum_kernel, [shape] * 2, [vmem()] * 5, [vmem()] * 2, [], 16 * own.size)(
        own, left_a, left_b, right_a, right_b
    )


def pad_kernel(table, keep, other_a, own, other_b, left_a, left_b, right_a, right_b, out, total):
    half = left_a.shape[0]
    rows_a = keep.shape[1]
    total[:, :rows_a] = keep[...] + other_a[...]
    lower, upper = slice(0, half), slice(half, None)
    for part, left, right in ((lower, left_a, right_a), (upper, left_b, right_b)):
        total[part, rows_a:] = (own[part] + other_b[3, part]) + (left[...] + right[...])

    def body(k, carry):
        s = table[k]

        @pl.when(s >= 0)
        def _():
            out[k] = total[s]

        @pl.when(s < 0)
        def _():
            out[k] = jnp.zeros_like(out[k])

        return carry

    lax.fori_loop(0, out.shape[0], body, 0)


def pad(table, *terms):
    slots, rows_a, width = terms[0].shape
    rows = rows_a + terms[2].shape[1]
    shape = jax.ShapeDtypeStruct((table.shape[0], rows, width), jnp.float32)
    scratch = [pltpu.VMEM((slots, rows, width), jnp.float32)]
    return call(
        pad_kernel, shape, [smem()] + [vmem()] * 8, vmem(), scratch, 24 * slots * rows * width
    )(table, *terms)


def to_owners(padded, groups):
    n, rows, width = padded.shape
    pieces = lax.all_to_all(padded.reshape(groups, n // groups, rows, width), "vir", 0, 0)
    return pieces.reshape(n, rows, width)


def finish_kernel(place, pieces, out, acc):
    acc[...] = jnp.zeros_like(acc)

    def body(k, carry):
        p = place[k]

        @pl.when(p >= 0)
        def _():
            acc[p] = acc[p] + pieces[k]

        return carry

    lax.fori_loop(0, pieces.shape[0], body, 0)
    tiles, _, width = acc.shape
    for c in range(tiles):
        out[:, c * width : (c + 1) * width] = acc[c]


def finish(place, pieces, tiles):
    _, rows, width = pieces.shape
    shape = jax.ShapeDtypeStruct((rows, tiles * width), jnp.float32)
    scratch = [pltpu.VMEM((tiles, rows, width), jnp.float32)]
    return call(finish_kernel, shape, [smem(), vmem()], vmem(), scratch, 4 * pieces.size)(
        place, pieces
    )


def routes(residual_list, owner_pos, tiles_dev, me):
    groups, slots = residual_list.shape
    total = owner_pos.shape[0]
    tiles = jnp.arange(total, dtype=jnp.int32)
    positions = jnp.sum(
        jnp.where(residual_list[:, :, None] == tiles, owner_pos, 0), axis=2, dtype=jnp.int32
    )
    owners = jnp.arange(groups, dtype=jnp.int32)
    index = jnp.arange(slots, dtype=jnp.int32)
    before = index[None, :] < index[:, None]

    def row(v):
        return jnp.sum(jnp.where(owners[:, None] == v, positions, 0), axis=0, dtype=jnp.int32)

    def pick(mask, value):
        rank = jnp.sum(mask[:, None, :] & before, axis=2, dtype=jnp.int32)
        chosen = mask[:, :, None] & (rank[:, :, None] == jnp.arange(2, dtype=jnp.int32))
        return jnp.max(jnp.where(chosen, value[:, :, None], -1), axis=1).reshape(-1)

    own = row(me)
    to_owner = (own // tiles_dev)[None, :] == owners[:, None]
    send = pick(to_owner, jnp.broadcast_to(index, (groups, slots)))
    place = pick(positions // tiles_dev == me, positions % tiles_dev)
    return send, place


def shards(t2, integral_tiles, contract_tile, slot_of_block, residual_list, owner_pos):
    width = integral_tiles.shape[-1]
    tiles_dev = t2.shape[1] // width
    groups, slots = residual_list.shape
    half = slots // 2
    rows_a = ROWS_A
    rows = t2.shape[0]
    rows_b = rows - rows_a

    me = lax.axis_index("vir")
    send, place = routes(residual_list, owner_pos, tiles_dev, me)
    offsets = [(dx, dy) for dy in (2, 1, -1, 0) for dx in (0, 1)]
    pieces = [from_occ(t2, dx, dy) if dx or dy else t2 for dx, dy in offsets]

    one = (slots, rows_b, width)
    shapes = [(2, half, rows_a, width)] * 6 + [(2, slots, rows_a, width)] + [one] * 4 + [(4,) + one]
    moves = []
    for g in range(4):
        for part in range(2) if g < 3 else (None,):
            for d in range(2):
                row = (2 * g + d) * rows
                if part is None:
                    moves.append((6, d, 0, slots, row, rows_a))
                else:
                    moves.append((2 * g + part, d, part * half, half, row, rows_a))
        moves.append((7 + g, None, 0, slots, 2 * g * rows + rows_a, rows_b))
        moves.append((11, g, 0, slots, (2 * g + 1) * rows + rows_a, rows_b))
    far_a, far_b, up_a, up_b, down_a, down_b, own, far, up, down, here, give_b = products(
        contract_tile, slot_of_block, integral_tiles[0], pieces, slots, shapes, moves
    )
    other_b = from_occ(give_b, 1, 0)
    left_far = from_occ(far_a, 0, -1)
    right_far = from_occ(far_b, 0, 1)
    left_b = from_occ(up_b, 0, -1)
    right_a = from_occ(down_a, 0, 1)
    left_a = from_occ(up_a + left_far, 0, -1)
    right_b = from_occ(down_b + right_far, 0, 1)
    sums_a = (own, left_a, left_b, right_a, right_b)

    left_far = from_occ(far[:half] + other_b[0, :half], 0, -1)
    right_far = from_occ(far[half:] + other_b[0, half:], 0, 1)
    left_b = from_occ(up[half:] + other_b[1, half:], 0, -1)
    right_a = from_occ(down[:half] + other_b[2, :half], 0, 1)
    left_a = from_occ(up[:half] + other_b[1, :half] + left_far, 0, -1)
    right_b = from_occ(down[half:] + other_b[2, half:] + right_far, 0, 1)

    keep, give = y_sum(*sums_a)
    other = from_occ(give, 1, 0)
    padded = pad(send, keep, other, here, other_b, left_a, left_b, right_a, right_b)
    return finish(place, to_owners(padded, groups), tiles_dev)


def solution(mesh):
    in_specs = (
        P("occ", "vir"),
        P("occ", "vir", None, None),
        P("occ", "vir"),
        P("occ", "vir"),
        P(),
        P(),
    )
    out_specs = P("occ", "vir")
    return jax.shard_map(shards, mesh=mesh, in_specs=in_specs, out_specs=out_specs, check_vma=False)
```

time: 382 us -> 178 us (0.47); the launches traced: 377 us -> 178 us
  waiting for transfers between devices: 272 us -> 103 us
  matrix products: 64.5 us -> 0 us
  starting transfers between devices: 0.08 us -> 46.7 us
  local copies, waits for them, and re-layouts: 25.8 us -> 1.13 us
  Pallas kernels: 0 us -> 21.3 us
  between operations: 13.1 us -> 0.18 us
  other arithmetic: 1.33 us -> 5.21 us
    reduce_scatter x1 -> x0, waiting for transfers between devices: 120 us -> none  [shards(): lax.psum_scatter(spread.reshape(rows_dev, tile_total * tile_width), 'vir'...]
    unnamed x4 -> x0, waiting for transfers between devices: 111 us -> none
    dot_general x3 -> x0, matrix products: 64.5 us -> none  [the longest x1 44.9 us: shards(): jnp.dot(gathered, dense_map, precision=highest, preferred_element_type=jn...]
    ppermute x0 -> x21, waiting for transfers between devices: none -> 51.7 us  [from_occ(): return lax.ppermute(v, 'occ', perm)]
    all_to_all x0 -> x1, waiting for transfers between devices: none -> 51.3 us  [to_owners(): lax.all_to_all(padded.reshape(groups, n // groups, rows, width), 'vir', 0...]
    all_gather x1 -> x0, waiting for transfers between devices: 41.7 us -> none  [shards(): gathered = lax.all_gather(t2, 'occ', axis=0, tiled=True)]
    ppermute x0 -> x21, starting transfers between devices: none -> 37 us  [from_occ(): return lax.ppermute(v, 'occ', perm)]
    pallas_call x0 -> x4, Pallas kernels: none -> 21.3 us  [the longest x1 14.3 us: products(): call(functools.partial(product_kernel, len(pieces), moves), shapes, [smem...]
  transfers between devices with their start and end apart: 3 -> 22, of which waited for: 3 -> 13; matrix products, arithmetic and copies ran while one was open for 7% -> 3% of each run, Pallas kernels for 0% -> 1%
where the time goes in v1:
time: 178 us
  waiting for transfers between devices  103 us (58%)
  starting transfers between devices  46.7 us (26%)
  Pallas kernels  21.3 us (12%)
  other arithmetic  5.21 us (3%)
    ppermute x21, waiting for transfers between devices, from_occ(): return lax.ppermute(v, 'occ', perm)  51.7 us
    all_to_all x1, waiting for transfers between devices, to_owners(): lax.all_to_all(padded.reshape(groups, n // groups, rows, width), 'vir', 0...  51.3 us
    ppermute x21, starting transfers between devices, from_occ(): return lax.ppermute(v, 'occ', perm)  37 us
    pallas_call x1, Pallas kernels, products(): call(functools.partial(product_kernel, len(pieces), moves), shapes, [smem...  14.3 us
    all_to_all x1, starting transfers between devices, to_owners(): lax.all_to_all(padded.reshape(groups, n // groups, rows, width), 'vir', 0...  9.71 us
    pallas_call x1, Pallas kernels, pad(): call(pad_kernel, shape, [smem()] + [vmem()] * 8, vmem(), scratch, 24 * sl...  3.81 us
  transfers between devices with their start and end apart: 22, of which 13 were waited for; matrix products, arithmetic and copies ran while one was open for 3% of the time, Pallas kernels for 1%

profile of v1, /device:TPU:32, one launch (start us, length us, event | category | flops | bytes accessed | tf_op | source)
XLA Modules:
  0.0 177.5 jit_solution(11586905066685500577)
XLA Ops:
  0.0 4.0 %collective-permute-start.5 = (f32[64,768]{1,0:T(8,128)}, f32[64,768]{1,0:T(8,128)S(1)}, u32[]{:S(2)}, u32[]{:S(2)}) collective-permute-start(f32[64,768]{1,0:T(8,128)} %refs_9_.1), channel_id=1, source_target_pairs={{224,0},{128,32},{160,64},{192,96},{96,128},{0,160},{32,192},{64,2... | collective-permute-start | bytes 589832 | tf_op jit(solution)/shard_map/ppermute | solution.py:24
  4.0 1.6 collective-permute-start.4
  5.6 1.6 collective-permute-start.3
  7.2 0.4 collective-permute-start.2
  7.7 4.4 %collective-permute-start.1 = (f32[64,768]{1,0:T(8,128)}, f32[64,768]{1,0:T(8,128)S(1)}, u32[]{:S(2)}, u32[]{:S(2)}) collective-permute-start(f32[64,768]{1,0:T(8,128)} %refs_9_.1), channel_id=1, source_target_pairs={{192,0},{224,32},{128,64},{160,96},{64,128},{96,160},{0,192},{32,2... | collective-permute-start | bytes 589832 | tf_op jit(solution)/shard_map/ppermute | solution.py:24
  12.1 1.5 collective-permute-start
  13.7 1.4 collective-permute-done.4.refs_7_
  15.1 1.6 collective-permute-start.6
  16.7 6.5 %collective-permute-done.2.refs_5_ = f32[64,768]{1,0:T(8,128)S(1)} collective-permute-done((f32[64,768]{1,0:T(8,128)}, f32[64,768]{1,0:T(8,128)S(1)}, u32[]{:S(2)}, u32[]{:S(2)}) %collective-permute-start.2) | collective-permute-done | bytes 196640 | tf_op jit(solution)/shard_map/ppermute | solution.py:24
  23.2 1.1 collective-permute-done.refs_3_
  24.4 0.6 copy-done.12
  25.0 0.1 copy-done.13
  25.1 14.3 %shard_map.64 = (f32[2,16,40,128]{3,2,1,0:T(8,128)}, f32[2,16,40,128]{3,2,1,0:T(8,128)}, f32[2,16,40,128]{3,2,1,0:T(8,128)}, f32[2,16,40,128]{3,2,1,0:T(8,128)},...) custom-call(s32[1,64]{1,0:T(1,128)} %refs_0_.1, ...), custom_call_target="tpu_custom_call" | custom-call | flops 4294967296 | bytes 14155776 | tf_op jit(solution)/shard_map/pallas_call | solution.py:128
  39.4 1.7 collective-permute-start.14
  41.2 4.0 %collective-permute-start.7 = (f32[2,16,40,128]{3,2,1,0:T(8,128)}, f32[2,16,40,128]{3,2,1,0:T(8,128)S(1)}, u32[]{:S(2)}, u32[]{:S(2)}) collective-permute-start(f32[2,16,40,128]{3,2,1,0:T(8,128)} %get-tuple-element.21), channel_id=1, source_target_pairs={{96,0},{0,32},{32,64},{64,96},{224,128},{128,160},{160,192},{192,2... | collective-permute-start | bytes 1966088 | tf_op jit(solution)/shard_map/ppermute | solution.py:24
  45.1 1.6 collective-permute-start.11
  46.7 1.5 select_reduce_fusion
  48.2 1.0 collective-permute-start.9
  49.2 2.3 %collective-permute-start.10 = (f32[2,16,40,128]{3,2,1,0:T(8,128)}, f32[2,16,40,128]{3,2,1,0:T(8,128)S(1)}, u32[]{:S(2)}, u32[]{:S(2)}) collective-permute-start(f32[2,16,40,128]{3,2,1,0:T(8,128)} %get-tuple-element.23), channel_id=1, source_target_pairs={{32,0},{64,32},{96,64},{0,96},{160,128},{192,160},{224,192},{128,2... | collective-permute-start | bytes 1966088 | tf_op jit(solution)/shard_map/ppermute | solution.py:24
  51.5 11.1 %collective-permute-done.7 = f32[2,16,40,128]{3,2,1,0:T(8,128)S(1)} collective-permute-done((f32[2,16,40,128]{3,2,1,0:T(8,128)}, f32[2,16,40,128]{3,2,1,0:T(8,128)S(1)}, u32[]{:S(2)}, u32[]{:S(2)}) %collective-permute-start.7) | collective-permute-done | bytes 655392 | tf_op jit(solution)/shard_map/ppermute | solution.py:24
  62.6 1.3 add.55
  63.8 0.8 collective-permute-start.8
  64.7 2.8 %collective-permute-start.12 = (f32[2,16,40,128]{3,2,1,0:T(8,128)S(1)}, f32[2,16,40,128]{3,2,1,0:T(8,128)S(1)}, u32[]{:S(2)}, u32[]{:S(2)}) collective-permute-start(f32[2,16,40,128]{3,2,1,0:T(8,128)S(1)} %add.56), channel_id=1, source_target_pairs={{32,0},{64,32},{96,64},{0,96},{160,128},{192,160},{224,192},{128,2... | collective-permute-start | bytes 1966088 | tf_op jit(solution)/shard_map/ppermute | solution.py:24
  67.5 0.1 select_reduce_fusion.3
  67.6 9.0 %collective-permute-done.9.left_b = f32[2,16,40,128]{3,2,1,0:T(8,128)S(1)} collective-permute-done((f32[2,16,40,128]{3,2,1,0:T(8,128)}, f32[2,16,40,128]{3,2,1,0:T(8,128)S(1)}, u32[]{:S(2)}, u32[]{:S(2)}) %collective-permute-start.9) | collective-permute-done | bytes 655392 | tf_op jit(solution)/shard_map/ppermute | solution.py:24
  76.6 0.9 collective-permute-done.10.right_a
  77.5 11.0 %collective-permute-done.8.left_a = f32[2,16,40,128]{3,2,1,0:T(8,128)S(1)} collective-permute-done((f32[2,16,40,128]{3,2,1,0:T(8,128)S(1)}, f32[2,16,40,128]{3,2,1,0:T(8,128)S(1)}, u32[]{:S(2)}, u32[]{:S(2)}) %collective-permute-start.8) | collective-permute-done | bytes 655392 | tf_op jit(solution)/shard_map/ppermute | solution.py:24
  88.6 1.0 shard_map.65
  89.6 0.4 collective-permute-start.13
  90.1 3.1 %collective-permute-start.19 = (f32[16,24,128]{2,1,0:T(8,128)S(1)}, f32[16,24,128]{2,1,0:T(8,128)S(1)}, u32[]{:S(2)}, u32[]{:S(2)}) collective-permute-start(f32[16,24,128]{2,1,0:T(8,128)S(1)} %get-tuple-element.37), channel_id=1, source_target_pairs={{32,0},{64,32},{96,64},{0,96},{160,128},{192,160},{224,192},{128,2... | collective-permute-start | bytes 589832 | tf_op jit(solution)/shard_map/ppermute | solution.py:24
  93.2 3.2 %collective-permute-done.19 = f32[16,24,128]{2,1,0:T(8,128)S(1)} collective-permute-done((f32[16,24,128]{2,1,0:T(8,128)S(1)}, f32[16,24,128]{2,1,0:T(8,128)S(1)}, u32[]{:S(2)}, u32[]{:S(2)}) %collective-permute-start.19) | collective-permute-done | bytes 196640 | tf_op jit(solution)/shard_map/ppermute | solution.py:24
  96.3 3.7 %collective-permute-done.15 = f32[16,24,128]{2,1,0:T(8,128)S(1)} collective-permute-done((f32[16,24,128]{2,1,0:T(8,128)S(1)}, f32[16,24,128]{2,1,0:T(8,128)S(1)}, u32[]{:S(2)}, u32[]{:S(2)}) %collective-permute-start.15) | collective-permute-done | bytes 196640 | tf_op jit(solution)/shard_map/ppermute | solution.py:24
  100.0 0.9 fusion.2
  101.0 2.0 %collective-permute-start.16 = (f32[16,24,128]{2,1,0:T(8,128)}, f32[16,24,128]{2,1,0:T(8,128)}, u32[]{:S(2)}, u32[]{:S(2)}) collective-permute-start(f32[16,24,128]{2,1,0:T(8,128)} %get-tuple-element.41), channel_id=1, source_target_pairs={{96,0},{0,32},{32,64},{64,96},{224,128},{128,160},{160,192},{192,2... | collective-permute-start | bytes 589832 | tf_op jit(solution)/shard_map/ppermute | solution.py:24
  103.0 2.0 %collective-permute-start.17 = (f32[16,24,128]{2,1,0:T(8,128)}, f32[16,24,128]{2,1,0:T(8,128)}, u32[]{:S(2)}, u32[]{:S(2)}) collective-permute-start(f32[16,24,128]{2,1,0:T(8,128)} %get-tuple-element.42), channel_id=1, source_target_pairs={{96,0},{0,32},{32,64},{64,96},{224,128},{128,160},{160,192},{192,2... | collective-permute-start | bytes 589832 | tf_op jit(solution)/shard_map/ppermute | solution.py:24
  105.0 1.2 convert_reduce_fusion
  106.2 0.2 select_reduce_fusion.1
  106.3 0.1 copy.8
  106.4 0.1 reshape.107.table
  106.5 0.3 collective-permute-done.20.right_b
  106.8 2.2 %collective-permute-done.18.right_a = f32[16,24,128]{2,1,0:T(8,128)} collective-permute-done((f32[16,24,128]{2,1,0:T(8,128)}, f32[16,24,128]{2,1,0:T(8,128)}, u32[]{:S(2)}, u32[]{:S(2)}) %collective-permute-start.18) | collective-permute-done | bytes 196640 | tf_op jit(solution)/shard_map/ppermute | solution.py:24
  109.1 1.3 collective-permute-done.17.left_b
  110.3 3.8 %shard_map.66 = f32[64,64,128]{2,1,0:T(8,128)} custom-call(s32[64]{0:T(128)S(1)} %reshape.107.table, f32[32,40,128]{2,1,0:T(8,128)S(1)} %get-tuple-element.26.keep, f32[32,40,128]{2,1,0:T(8,128)S(1)} %collective-permute-done.13.other_a, f32[32,24,128]{2,1,0:T(8,128)S(1)} %copy-done.1, f32[4,32,24,128]{3,2,1,0:T(8,128)S(1)} %collective-permute-done.14.other_b, ...), custom_call_target="tpu_custom_call" | custom-call | bytes 6291456 | tf_op jit(solution)/shard_map/pallas_call | solution.py:191
  114.1 9.7 %all-to-all-start = ((f32[32,2,64,128]{3,2,1,0:T(8,128)}), f32[32,2,64,128]{3,2,1,0:T(8,128)S(1)}, u32[]{:S(2)}, u32[]{:S(2)}) async-start(f32[32,2,64,128]{3,2,1,0:T(8,128)} %bitcast.7), calls=%async_computation | async-start | bytes 4194304 | tf_op jit(solution)/shard_map/all_to_all | solution.py:198
  123.9 0.1 copy.7
  123.9 0.1 reshape.106.place
  124.1 51.3 %all-to-all-done = f32[32,2,64,128]{3,2,1,0:T(8,128)S(1)} async-done(((f32[32,2,64,128]{3,2,1,0:T(8,128)}), f32[32,2,64,128]{3,2,1,0:T(8,128)S(1)}, u32[]{:S(2)}, u32[]{:S(2)}) %all-to-all-start) | async-done | bytes 2097184 | tf_op jit(solution)/shard_map/all_to_all | solution.py:198
  175.3 2.2 %shard_map.67 = f32[64,768]{1,0:T(8,128)} custom-call(s32[64]{0:T(128)S(1)} %reshape.106.place, f32[64,64,128]{2,1,0:T(8,128)S(1)} %bitcast.31), custom_call_target="tpu_custom_call" | custom-call | bytes 2097152 | tf_op jit(solution)/shard_map/pallas_call | solution.py:224
  (45 shorter events, 0.3 us)
Async XLA Ops:
  0.0 12.1 %collective-permute-start.5 = (f32[64,768]{1,0:T(8,128)}, f32[64,768]{1,0:T(8,128)S(1)}, u32[]{:S(2)}, u32[]{:S(2)}) collective-permute-start(f32[64,768]{1,0:T(8,128)} %refs_9_.1), channel_id=1, source_target_pairs={{224,0},{128,32},{160,64},{192,96},{96,128},{0,160},{32,192},{64,2... | collective-permute-start | bytes 589832 | tf_op jit(solution)/shard_map/ppermute | solution.py:24
  4.0 11.0 %collective-permute-start.4 = (f32[64,768]{1,0:T(8,128)}, f32[64,768]{1,0:T(8,128)S(1)}, u32[]{:S(2)}, u32[]{:S(2)}) collective-permute-start(f32[64,768]{1,0:T(8,128)} %refs_9_.1), channel_id=1, source_target_pairs={{96,0},{0,32},{32,64},{64,96},{224,128},{128,160},{160,192},{192,2... | collective-permute-start | bytes 589832 | tf_op jit(solution)/shard_map/ppermute | solution.py:24
  5.6 11.1 %collective-permute-start.3 = (f32[64,768]{1,0:T(8,128)}, f32[64,768]{1,0:T(8,128)S(1)}, u32[]{:S(2)}, u32[]{:S(2)}) collective-permute-start(f32[64,768]{1,0:T(8,128)} %refs_9_.1), channel_id=1, source_target_pairs={{160,0},{192,32},{224,64},{128,96},{32,128},{64,160},{96,192},{0,2... | collective-permute-start | bytes 589832 | tf_op jit(solution)/shard_map/ppermute | solution.py:24
  7.2 16.0 %collective-permute-start.2 = (f32[64,768]{1,0:T(8,128)}, f32[64,768]{1,0:T(8,128)S(1)}, u32[]{:S(2)}, u32[]{:S(2)}) collective-permute-start(f32[64,768]{1,0:T(8,128)} %refs_9_.1), channel_id=1, source_target_pairs={{32,0},{64,32},{96,64},{0,96},{160,128},{192,160},{224,192},{128,2... | collective-permute-start | bytes 589832 | tf_op jit(solution)/shard_map/ppermute | solution.py:24
  7.7 15.5 %collective-permute-start.1 = (f32[64,768]{1,0:T(8,128)}, f32[64,768]{1,0:T(8,128)S(1)}, u32[]{:S(2)}, u32[]{:S(2)}) collective-permute-start(f32[64,768]{1,0:T(8,128)} %refs_9_.1), channel_id=1, source_target_pairs={{192,0},{224,32},{128,64},{160,96},{64,128},{96,160},{0,192},{32,2... | collective-permute-start | bytes 589832 | tf_op jit(solution)/shard_map/ppermute | solution.py:24
  12.1 12.2 %copy-start.7 = (f32[64,768]{1,0:T(8,128)}, f32[64,768]{1,0:T(8,128)S(1)}, u32[]{:S(2)}) copy-start(f32[64,768]{1,0:T(8,128)S(1)} %collective-permute-done.5.refs_8_) | copy-start | bytes 589828
  12.1 12.2 %collective-permute-start = (f32[64,768]{1,0:T(8,128)}, f32[64,768]{1,0:T(8,128)S(1)}, u32[]{:S(2)}, u32[]{:S(2)}) collective-permute-start(f32[64,768]{1,0:T(8,128)} %refs_9_.1), channel_id=1, source_target_pairs={{64,0},{96,32},{0,64},{32,96},{192,128},{224,160},{128,192},{160,2... | collective-permute-start | bytes 589832 | tf_op jit(solution)/shard_map/ppermute | solution.py:24
  15.1 9.3 %copy-start.8 = (f32[64,768]{1,0:T(8,128)}, f32[64,768]{1,0:T(8,128)S(1)}, u32[]{:S(2)}) copy-start(f32[64,768]{1,0:T(8,128)S(1)} %collective-permute-done.4.refs_7_) | copy-start | bytes 589828
  15.1 9.3 %collective-permute-start.6 = (f32[64,768]{1,0:T(8,128)}, f32[64,768]{1,0:T(8,128)S(1)}, u32[]{:S(2)}, u32[]{:S(2)}) collective-permute-start(f32[64,768]{1,0:T(8,128)} %refs_9_.1), channel_id=1, source_target_pairs={{128,0},{160,32},{192,64},{224,96},{0,128},{32,160},{64,192},{96,2... | collective-permute-start | bytes 589832 | tf_op jit(solution)/shard_map/ppermute | solution.py:24
  16.7 7.7 %copy-start.9 = (f32[64,768]{1,0:T(8,128)}, f32[64,768]{1,0:T(8,128)S(1)}, u32[]{:S(2)}) copy-start(f32[64,768]{1,0:T(8,128)S(1)} %collective-permute-done.3.refs_6_) | copy-start | bytes 589828
  23.2 1.2 copy-start.10
  23.2 1.2 copy-start.11
  24.3 0.7 copy-start.12
  24.4 0.7 copy-start.13
  25.1 21.6 %copy-start.6 = (s32[32,32]{1,0:T(8,128)S(1)}, s32[32,32]{1,0:T(8,128)}, u32[]{:S(2)}) copy-start(s32[32,32]{1,0:T(8,128)} %param.10) | copy-start | bytes 12292
  39.4 25.2 %copy-start.2 = (f32[2,16,40,128]{3,2,1,0:T(8,128)S(1)}, f32[2,16,40,128]{3,2,1,0:T(8,128)}, u32[]{:S(2)}) copy-start(f32[2,16,40,128]{3,2,1,0:T(8,128)} %get-tuple-element.24) | copy-start | bytes 1966084
  39.4 50.6 %collective-permute-start.14 = (f32[4,32,24,128]{3,2,1,0:T(8,128)}, f32[4,32,24,128]{3,2,1,0:T(8,128)S(1)}, u32[]{:S(2)}, u32[]{:S(2)}) collective-permute-start(f32[4,32,24,128]{3,2,1,0:T(8,128)} %get-tuple-element.29), channel_id=1, source_target_pairs={{128,0},{160,32},{192,64},{224,96},{0,128},{32,160},{64,192},{96,2... | collective-permute-start | bytes 4718600 | tf_op jit(solution)/shard_map/ppermute | solution.py:24
  41.2 21.4 %collective-permute-start.7 = (f32[2,16,40,128]{3,2,1,0:T(8,128)}, f32[2,16,40,128]{3,2,1,0:T(8,128)S(1)}, u32[]{:S(2)}, u32[]{:S(2)}) collective-permute-start(f32[2,16,40,128]{3,2,1,0:T(8,128)} %get-tuple-element.21), channel_id=1, source_target_pairs={{96,0},{0,32},{32,64},{64,96},{224,128},{128,160},{160,192},{192,2... | collective-permute-start | bytes 1966088 | tf_op jit(solution)/shard_map/ppermute | solution.py:24
  45.1 19.5 %collective-permute-start.11 = (f32[2,16,40,128]{3,2,1,0:T(8,128)}, f32[2,16,40,128]{3,2,1,0:T(8,128)S(1)}, u32[]{:S(2)}, u32[]{:S(2)}) collective-permute-start(f32[2,16,40,128]{3,2,1,0:T(8,128)} %get-tuple-element.25), channel_id=1, source_target_pairs={{32,0},{64,32},{96,64},{0,96},{160,128},{192,160},{224,192},{128,2... | collective-permute-start | bytes 1966088 | tf_op jit(solution)/shard_map/ppermute | solution.py:24
  48.2 28.4 %collective-permute-start.9 = (f32[2,16,40,128]{3,2,1,0:T(8,128)}, f32[2,16,40,128]{3,2,1,0:T(8,128)S(1)}, u32[]{:S(2)}, u32[]{:S(2)}) collective-permute-start(f32[2,16,40,128]{3,2,1,0:T(8,128)} %get-tuple-element.22), channel_id=1, source_target_pairs={{96,0},{0,32},{32,64},{64,96},{224,128},{128,160},{160,192},{192,2... | collective-permute-start | bytes 1966088 | tf_op jit(solution)/shard_map/ppermute | solution.py:24
  49.2 28.3 %collective-permute-start.10 = (f32[2,16,40,128]{3,2,1,0:T(8,128)}, f32[2,16,40,128]{3,2,1,0:T(8,128)S(1)}, u32[]{:S(2)}, u32[]{:S(2)}) collective-permute-start(f32[2,16,40,128]{3,2,1,0:T(8,128)} %get-tuple-element.23), channel_id=1, source_target_pairs={{32,0},{64,32},{96,64},{0,96},{160,128},{192,160},{224,192},{128,2... | collective-permute-start | bytes 1966088 | tf_op jit(solution)/shard_map/ppermute | solution.py:24
  62.6 26.0 %copy-start = (f32[2,32,40,128]{3,2,1,0:T(8,128)S(1)}, f32[2,32,40,128]{3,2,1,0:T(8,128)}, u32[]{:S(2)}) copy-start(f32[2,32,40,128]{3,2,1,0:T(8,128)} %get-tuple-element.19.own) | copy-start | bytes 3932164
  63.8 24.7 %collective-permute-start.8 = (f32[2,16,40,128]{3,2,1,0:T(8,128)S(1)}, f32[2,16,40,128]{3,2,1,0:T(8,128)S(1)}, u32[]{:S(2)}, u32[]{:S(2)}) collective-permute-start(f32[2,16,40,128]{3,2,1,0:T(8,128)S(1)} %add.55), channel_id=1, source_target_pairs={{96,0},{0,32},{32,64},{64,96},{224,128},{128,160},{160,192},{192,2... | collective-permute-start | bytes 1966088 | tf_op jit(solution)/shard_map/ppermute | solution.py:24
  64.7 23.8 %collective-permute-start.12 = (f32[2,16,40,128]{3,2,1,0:T(8,128)S(1)}, f32[2,16,40,128]{3,2,1,0:T(8,128)S(1)}, u32[]{:S(2)}, u32[]{:S(2)}) collective-permute-start(f32[2,16,40,128]{3,2,1,0:T(8,128)S(1)} %add.56), channel_id=1, source_target_pairs={{32,0},{64,32},{96,64},{0,96},{160,128},{192,160},{224,192},{128,2... | collective-permute-start | bytes 1966088 | tf_op jit(solution)/shard_map/ppermute | solution.py:24
  88.6 1.4 copy-start.3
  88.6 11.5 %copy-start.4 = (f32[32,24,128]{2,1,0:T(8,128)S(1)}, f32[32,24,128]{2,1,0:T(8,128)}, u32[]{:S(2)}) copy-start(f32[32,24,128]{2,1,0:T(8,128)} %get-tuple-element.30) | copy-start | bytes 1179652
  88.6 11.5 %copy-start.5 = (f32[32,24,128]{2,1,0:T(8,128)S(1)}, f32[32,24,128]{2,1,0:T(8,128)}, u32[]{:S(2)}) copy-start(f32[32,24,128]{2,1,0:T(8,128)} %get-tuple-element.32) | copy-start | bytes 1179652
  89.6 16.9 %collective-permute-start.13 = (f32[32,40,128]{2,1,0:T(8,128)}, f32[32,40,128]{2,1,0:T(8,128)S(1)}, u32[]{:S(2)}, u32[]{:S(2)}) collective-permute-start(f32[32,40,128]{2,1,0:T(8,128)} %get-tuple-element.27), channel_id=1, source_target_pairs={{128,0},{160,32},{192,64},{224,96},{0,128},{32,160},{64,192},{96,2... | collective-permute-start | bytes 1966088 | tf_op jit(solution)/shard_map/ppermute | solution.py:24
  90.0 20.3 %copy-start.1 = (f32[32,24,128]{2,1,0:T(8,128)S(1)}, f32[32,24,128]{2,1,0:T(8,128)}, u32[]{:S(2)}) copy-start(f32[32,24,128]{2,1,0:T(8,128)} %get-tuple-element.28.own) | copy-start | bytes 1179652
  90.1 6.3 %collective-permute-start.19 = (f32[16,24,128]{2,1,0:T(8,128)S(1)}, f32[16,24,128]{2,1,0:T(8,128)S(1)}, u32[]{:S(2)}, u32[]{:S(2)}) collective-permute-start(f32[16,24,128]{2,1,0:T(8,128)S(1)} %get-tuple-element.37), channel_id=1, source_target_pairs={{32,0},{64,32},{96,64},{0,96},{160,128},{192,160},{224,192},{128,2... | collective-permute-start | bytes 589832 | tf_op jit(solution)/shard_map/ppermute | solution.py:24
  93.2 6.9 %collective-permute-start.15 = (f32[16,24,128]{2,1,0:T(8,128)S(1)}, f32[16,24,128]{2,1,0:T(8,128)S(1)}, u32[]{:S(2)}, u32[]{:S(2)}) collective-permute-start(f32[16,24,128]{2,1,0:T(8,128)S(1)} %get-tuple-element.38), channel_id=1, source_target_pairs={{96,0},{0,32},{32,64},{64,96},{224,128},{128,160},{160,192},{192,2... | collective-permute-start | bytes 589832 | tf_op jit(solution)/shard_map/ppermute | solution.py:24
  101.0 5.9 %collective-permute-start.20 = (f32[16,24,128]{2,1,0:T(8,128)}, f32[16,24,128]{2,1,0:T(8,128)S(1)}, u32[]{:S(2)}, u32[]{:S(2)}) collective-permute-start(f32[16,24,128]{2,1,0:T(8,128)} %get-tuple-element.35), channel_id=1, source_target_pairs={{32,0},{64,32},{96,64},{0,96},{160,128},{192,160},{224,192},{128,2... | collective-permute-start | bytes 589832 | tf_op jit(solution)/shard_map/ppermute | solution.py:24
  101.0 8.1 %collective-permute-start.18 = (f32[16,24,128]{2,1,0:T(8,128)}, f32[16,24,128]{2,1,0:T(8,128)}, u32[]{:S(2)}, u32[]{:S(2)}) collective-permute-start(f32[16,24,128]{2,1,0:T(8,128)} %get-tuple-element.36), channel_id=1, source_target_pairs={{32,0},{64,32},{96,64},{0,96},{160,128},{192,160},{224,192},{128,2... | collective-permute-start | bytes 589832 | tf_op jit(solution)/shard_map/ppermute | solution.py:24
  101.0 8.1 %collective-permute-start.16 = (f32[16,24,128]{2,1,0:T(8,128)}, f32[16,24,128]{2,1,0:T(8,128)}, u32[]{:S(2)}, u32[]{:S(2)}) collective-permute-start(f32[16,24,128]{2,1,0:T(8,128)} %get-tuple-element.41), channel_id=1, source_target_pairs={{96,0},{0,32},{32,64},{64,96},{224,128},{128,160},{160,192},{192,2... | collective-permute-start | bytes 589832 | tf_op jit(solution)/shard_map/ppermute | solution.py:24
  103.0 7.3 %collective-permute-start.17 = (f32[16,24,128]{2,1,0:T(8,128)}, f32[16,24,128]{2,1,0:T(8,128)}, u32[]{:S(2)}, u32[]{:S(2)}) collective-permute-start(f32[16,24,128]{2,1,0:T(8,128)} %get-tuple-element.42), channel_id=1, source_target_pairs={{96,0},{0,32},{32,64},{64,96},{224,128},{128,160},{160,192},{192,2... | collective-permute-start | bytes 589832 | tf_op jit(solution)/shard_map/ppermute | solution.py:24
  114.1 61.2 %all-to-all-start = ((f32[32,2,64,128]{3,2,1,0:T(8,128)}), f32[32,2,64,128]{3,2,1,0:T(8,128)S(1)}, u32[]{:S(2)}, u32[]{:S(2)}) async-start(f32[32,2,64,128]{3,2,1,0:T(8,128)} %bitcast.7), calls=%async_computation | async-start | bytes 4194304 | tf_op jit(solution)/shard_map/all_to_all | solution.py:198

commit v2 on v1

--- a/solution.py
+++ b/solution.py
@@ -159,28 +159,17 @@
     )
 
 
-def pad_kernel(table, keep, other_a, own, other_b, left_a, left_b, right_a, right_b, out, total):
-    half = left_a.shape[0]
+def pad_kernel(table, keep, other_a, own, other_b, far, up, down, out, total):
     rows_a = keep.shape[1]
     total[:, :rows_a] = keep[...] + other_a[...]
-    lower, upper = slice(0, half), slice(half, None)
-    for part, left, right in ((lower, left_a, right_a), (upper, left_b, right_b)):
-        total[part, rows_a:] = (own[part] + other_b[3, part]) + (left[...] + right[...])
+    total[:, rows_a:] = (own[...] + other_b[3]) + (far[...] + (up[...] + down[...]))
 
     def body(k, carry):
         s = table[k]
-
-        @pl.when(s >= 0)
-        def _():
-            out[k] = total[s]
-
-        @pl.when(s < 0)
-        def _():
-            out[k] = jnp.zeros_like(out[k])
-
+        out[k] = jnp.where(s >= 0, total[jnp.maximum(s, 0)], 0.0)
         return carry
 
-    lax.fori_loop(0, out.shape[0], body, 0)
+    lax.fori_loop(0, out.shape[0], body, 0, unroll=8)
 
 
 def pad(table, *terms):
@@ -189,7 +178,7 @@
     shape = jax.ShapeDtypeStruct((table.shape[0], rows, width), jnp.float32)
     scratch = [pltpu.VMEM((slots, rows, width), jnp.float32)]
     return call(
-        pad_kernel, shape, [smem()] + [vmem()] * 8, vmem(), scratch, 24 * slots * rows * width
+        pad_kernel, shape, [smem()] + [vmem()] * 7, vmem(), scratch, 24 * slots * rows * width
     )(table, *terms)
 
 
@@ -204,14 +193,11 @@
 
     def body(k, carry):
         p = place[k]
-
-        @pl.when(p >= 0)
-        def _():
-            acc[p] = acc[p] + pieces[k]
-
+        tile = jnp.maximum(p, 0)
+        acc[tile] = acc[tile] + jnp.where(p >= 0, pieces[k], 0.0)
         return carry
 
-    lax.fori_loop(0, pieces.shape[0], body, 0)
+    lax.fori_loop(0, pieces.shape[0], body, 0, unroll=8)
     tiles, _, width = acc.shape
     for c in range(tiles):
         out[:, c * width : (c + 1) * width] = acc[c]
@@ -291,16 +277,13 @@
     right_b = from_occ(down_b + right_far, 0, 1)
     sums_a = (own, left_a, left_b, right_a, right_b)
 
-    left_far = from_occ(far[:half] + other_b[0, :half], 0, -1)
-    right_far = from_occ(far[half:] + other_b[0, half:], 0, 1)
-    left_b = from_occ(up[half:] + other_b[1, half:], 0, -1)
-    right_a = from_occ(down[:half] + other_b[2, :half], 0, 1)
-    left_a = from_occ(up[:half] + other_b[1, :half] + left_far, 0, -1)
-    right_b = from_occ(down[half:] + other_b[2, half:] + right_far, 0, 1)
+    from_far = from_occ(far + other_b[0], 0, 2)
+    from_down = from_occ(up + other_b[1], 0, -1)
+    from_up = from_occ(down + other_b[2], 0, 1)
 
     keep, give = y_sum(*sums_a)
     other = from_occ(give, 1, 0)
-    padded = pad(send, keep, other, here, other_b, left_a, left_b, right_a, right_b)
+    padded = pad(send, keep, other, here, other_b, from_far, from_down, from_up)
     return finish(place, to_owners(padded, groups), tiles_dev)
 
 

time: 178 us -> 171 us (0.961)
  starting transfers between devices: 46.7 us -> 43 us
  waiting for transfers between devices: 103 us -> 101 us
    ppermute x21 -> x18, starting transfers between devices: 37 us -> 33 us  [from_occ(): return lax.ppermute(v, 'occ', perm)]
    ppermute x21 -> x18, waiting for transfers between devices: 51.7 us -> 50.2 us  [from_occ(): return lax.ppermute(v, 'occ', perm)]
  transfers between devices with their start and end apart: 22 -> 19, of which waited for: 13 -> 11; matrix products, arithmetic and copies ran while one was open for 3% -> 3% of each run, Pallas kernels for 1% -> 1%
where the time goes in v2:
time: 171 us
  waiting for transfers between devices  101 us (59%)
  starting transfers between devices  43 us (25%)
  Pallas kernels  20.1 us (12%)
  other arithmetic  5.31 us (3%)
    all_to_all x1, waiting for transfers between devices, to_owners(): lax.all_to_all(padded.reshape(groups, n // groups, rows, width), 'vir', 0...  51.3 us
    ppermute x18, waiting for transfers between devices, from_occ(): return lax.ppermute(v, 'occ', perm)  50.2 us
    ppermute x18, starting transfers between devices, from_occ(): return lax.ppermute(v, 'occ', perm)  33 us
    pallas_call x1, Pallas kernels, products(): call(functools.partial(product_kernel, len(pieces), moves), shapes, [smem...  14.3 us
    all_to_all x1, starting transfers between devices, to_owners(): lax.all_to_all(padded.reshape(groups, n // groups, rows, width), 'vir', 0...  10 us
  transfers between devices with their start and end apart: 19, of which 11 were waited for; matrix products, arithmetic and copies ran while one was open for 3% of the time, Pallas kernels for 1%

profile of v2, /device:TPU:32, one launch (start us, length us, event | category | flops | bytes accessed | tf_op | source)
XLA Modules:
  0.0 171.1 jit_solution(407340365500999852)
XLA Ops:
  0.0 3.2 %collective-permute-start = (f32[64,768]{1,0:T(8,128)}, f32[64,768]{1,0:T(8,128)S(1)}, u32[]{:S(2)}, u32[]{:S(2)}) collective-permute-start(f32[64,768]{1,0:T(8,128)} %refs_9_.1), channel_id=1, source_target_pairs={{64,0},{96,32},{0,64},{32,96},{192,128},{224,160},{128,192},{160,2... | collective-permute-start | bytes 589832 | tf_op jit(solution)/shard_map/ppermute | solution.py:24
  3.2 2.8 %collective-permute-start.1 = (f32[64,768]{1,0:T(8,128)}, f32[64,768]{1,0:T(8,128)S(1)}, u32[]{:S(2)}, u32[]{:S(2)}) collective-permute-start(f32[64,768]{1,0:T(8,128)} %refs_9_.1), channel_id=1, source_target_pairs={{192,0},{224,32},{128,64},{160,96},{64,128},{96,160},{0,192},{32,2... | collective-permute-start | bytes 589832 | tf_op jit(solution)/shard_map/ppermute | solution.py:24
  6.0 3.0 %collective-permute-start.2 = (f32[64,768]{1,0:T(8,128)}, f32[64,768]{1,0:T(8,128)S(1)}, u32[]{:S(2)}, u32[]{:S(2)}) collective-permute-start(f32[64,768]{1,0:T(8,128)} %refs_9_.1), channel_id=1, source_target_pairs={{32,0},{64,32},{96,64},{0,96},{160,128},{192,160},{224,192},{128,2... | collective-permute-start | bytes 589832 | tf_op jit(solution)/shard_map/ppermute | solution.py:24
  9.0 0.7 collective-permute-start.3
  9.7 1.3 collective-permute-start.4
  11.0 2.1 %collective-permute-done.refs_3_ = f32[64,768]{1,0:T(8,128)S(1)} collective-permute-done((f32[64,768]{1,0:T(8,128)}, f32[64,768]{1,0:T(8,128)S(1)}, u32[]{:S(2)}, u32[]{:S(2)}) %collective-permute-start) | collective-permute-done | bytes 196640 | tf_op jit(solution)/shard_map/ppermute | solution.py:24
  13.1 8.5 %collective-permute-start.5 = (f32[64,768]{1,0:T(8,128)}, f32[64,768]{1,0:T(8,128)S(1)}, u32[]{:S(2)}, u32[]{:S(2)}) collective-permute-start(f32[64,768]{1,0:T(8,128)} %refs_9_.1), channel_id=1, source_target_pairs={{224,0},{128,32},{160,64},{192,96},{96,128},{0,160},{32,192},{64,2... | collective-permute-start | bytes 589832 | tf_op jit(solution)/shard_map/ppermute | solution.py:24
  21.6 0.0 collective-permute-done.1.refs_4_
  21.6 0.0 collective-permute-start.6
  21.6 0.0 collective-permute-done.4.refs_7_
  21.6 5.6 %collective-permute-done.5.refs_8_ = f32[64,768]{1,0:T(8,128)S(1)} collective-permute-done((f32[64,768]{1,0:T(8,128)}, f32[64,768]{1,0:T(8,128)S(1)}, u32[]{:S(2)}, u32[]{:S(2)}) %collective-permute-start.5) | collective-permute-done | bytes 196640 | tf_op jit(solution)/shard_map/ppermute | solution.py:24
  27.3 1.7 collective-permute-done.6.refs_10_
  29.0 0.6 copy-done.13
  29.6 14.3 %shard_map.64 = (f32[2,16,40,128]{3,2,1,0:T(8,128)}, f32[2,16,40,128]{3,2,1,0:T(8,128)}, f32[2,16,40,128]{3,2,1,0:T(8,128)}, f32[2,16,40,128]{3,2,1,0:T(8,128)},...) custom-call(s32[1,64]{1,0:T(1,128)} %refs_0_.1, ...), custom_call_target="tpu_custom_call" | custom-call | flops 4294967296 | bytes 14155776 | tf_op jit(solution)/shard_map/pallas_call | solution.py:128
  44.0 2.2 %collective-permute-start.14 = (f32[4,32,24,128]{3,2,1,0:T(8,128)}, f32[4,32,24,128]{3,2,1,0:T(8,128)S(1)}, u32[]{:S(2)}, u32[]{:S(2)}) collective-permute-start(f32[4,32,24,128]{3,2,1,0:T(8,128)} %get-tuple-element.29), channel_id=1, source_target_pairs={{128,0},{160,32},{192,64},{224,96},{0,128},{32,160},{64,192},{96,2... | collective-permute-start | bytes 4718600 | tf_op jit(solution)/shard_map/ppermute | solution.py:24
  46.2 1.3 collective-permute-start.11
  47.4 0.8 collective-permute-start.7
  48.2 1.5 select_reduce_fusion
  49.7 2.6 %collective-permute-start.10 = (f32[2,16,40,128]{3,2,1,0:T(8,128)}, f32[2,16,40,128]{3,2,1,0:T(8,128)S(1)}, u32[]{:S(2)}, u32[]{:S(2)}) collective-permute-start(f32[2,16,40,128]{3,2,1,0:T(8,128)} %get-tuple-element.23), channel_id=1, source_target_pairs={{32,0},{64,32},{96,64},{0,96},{160,128},{192,160},{224,192},{128,2... | collective-permute-start | bytes 1966088 | tf_op jit(solution)/shard_map/ppermute | solution.py:24
  52.2 0.0 collective-permute-start.9
  52.2 11.8 %collective-permute-done.11 = f32[2,16,40,128]{3,2,1,0:T(8,128)S(1)} collective-permute-done((f32[2,16,40,128]{3,2,1,0:T(8,128)}, f32[2,16,40,128]{3,2,1,0:T(8,128)S(1)}, u32[]{:S(2)}, u32[]{:S(2)}) %collective-permute-start.11) | collective-permute-done | bytes 655392 | tf_op jit(solution)/shard_map/ppermute | solution.py:24
  64.1 1.3 add.41
  65.3 2.7 %collective-permute-start.12 = (f32[2,16,40,128]{3,2,1,0:T(8,128)S(1)}, f32[2,16,40,128]{3,2,1,0:T(8,128)S(1)}, u32[]{:S(2)}, u32[]{:S(2)}) collective-permute-start(f32[2,16,40,128]{3,2,1,0:T(8,128)S(1)} %add.41), channel_id=1, source_target_pairs={{32,0},{64,32},{96,64},{0,96},{160,128},{192,160},{224,192},{128,2... | collective-permute-start | bytes 1966088 | tf_op jit(solution)/shard_map/ppermute | solution.py:24
  68.1 0.1 add.40
  68.1 0.1 collective-permute-start.8
  68.2 0.1 select_reduce_fusion.3
  68.4 8.6 %collective-permute-done.10.right_a = f32[2,16,40,128]{3,2,1,0:T(8,128)S(1)} collective-permute-done((f32[2,16,40,128]{3,2,1,0:T(8,128)}, f32[2,16,40,128]{3,2,1,0:T(8,128)S(1)}, u32[]{:S(2)}, u32[]{:S(2)}) %collective-permute-start.10) | collective-permute-done | bytes 655392 | tf_op jit(solution)/shard_map/ppermute | solution.py:24
  77.0 3.6 %collective-permute-done.9.left_b = f32[2,16,40,128]{3,2,1,0:T(8,128)S(1)} collective-permute-done((f32[2,16,40,128]{3,2,1,0:T(8,128)}, f32[2,16,40,128]{3,2,1,0:T(8,128)S(1)}, u32[]{:S(2)}, u32[]{:S(2)}) %collective-permute-start.9) | collective-permute-done | bytes 655392 | tf_op jit(solution)/shard_map/ppermute | solution.py:24
  80.6 3.9 %collective-permute-done.12.right_b = f32[2,16,40,128]{3,2,1,0:T(8,128)S(1)} collective-permute-done((f32[2,16,40,128]{3,2,1,0:T(8,128)S(1)}, f32[2,16,40,128]{3,2,1,0:T(8,128)S(1)}, u32[]{:S(2)}, u32[]{:S(2)}) %collective-permute-start.12) | collective-permute-done | bytes 655392 | tf_op jit(solution)/shard_map/ppermute | solution.py:24
  84.5 3.4 %collective-permute-done.8.left_a = f32[2,16,40,128]{3,2,1,0:T(8,128)S(1)} collective-permute-done((f32[2,16,40,128]{3,2,1,0:T(8,128)S(1)}, f32[2,16,40,128]{3,2,1,0:T(8,128)S(1)}, u32[]{:S(2)}, u32[]{:S(2)}) %collective-permute-start.8) | collective-permute-done | bytes 655392 | tf_op jit(solution)/shard_map/ppermute | solution.py:24
  87.9 1.0 shard_map.65
  89.0 0.7 collective-permute-start.13
  89.6 0.0 collective-permute-done.14.other_b
  89.6 1.1 fusion
  90.7 1.2 collective-permute-start.16
  91.9 2.1 %collective-permute-start.17 = (f32[32,24,128]{2,1,0:T(8,128)}, f32[32,24,128]{2,1,0:T(8,128)}, u32[]{:S(2)}, u32[]{:S(2)}) collective-permute-start(f32[32,24,128]{2,1,0:T(8,128)} %get-tuple-element.35), channel_id=1, source_target_pairs={{32,0},{64,32},{96,64},{0,96},{160,128},{192,160},{224,192},{128,2... | collective-permute-start | bytes 1179656 | tf_op jit(solution)/shard_map/ppermute | solution.py:24
  94.0 1.2 convert_reduce_fusion
  95.1 0.2 select_reduce_fusion.1
  95.3 0.1 copy.8
  95.4 0.1 reshape.107.table
  95.5 5.8 %collective-permute-done.13.other_a = f32[32,40,128]{2,1,0:T(8,128)S(1)} collective-permute-done((f32[32,40,128]{2,1,0:T(8,128)}, f32[32,40,128]{2,1,0:T(8,128)S(1)}, u32[]{:S(2)}, u32[]{:S(2)}) %collective-permute-start.13) | collective-permute-done | bytes 655392 | tf_op jit(solution)/shard_map/ppermute | solution.py:24
  101.3 3.6 %collective-permute-done.16.up = f32[32,24,128]{2,1,0:T(8,128)} collective-permute-done((f32[32,24,128]{2,1,0:T(8,128)}, f32[32,24,128]{2,1,0:T(8,128)}, u32[]{:S(2)}, u32[]{:S(2)}) %collective-permute-start.16) | collective-permute-done | bytes 393248 | tf_op jit(solution)/shard_map/ppermute | solution.py:24
  104.9 3.0 %shard_map.66 = f32[64,64,128]{2,1,0:T(8,128)} custom-call(s32[64]{0:T(128)S(1)} %reshape.107.table, f32[32,40,128]{2,1,0:T(8,128)S(1)} %get-tuple-element.26.keep, f32[32,40,128]{2,1,0:T(8,128)S(1)} %collective-permute-done.13.other_a, f32[32,24,128]{2,1,0:T(8,128)S(1)} %copy-done.1, f32[4,32,24,128]{3,2,1,0:T(8,128)S(1)} %collective-permute-done.14.other_b, ...), custom_call_target="tpu_custom_call" | custom-call | bytes 6291456 | tf_op jit(solution)/shard_map/pallas_call | solution.py:180
  107.9 10.0 %all-to-all-start = ((f32[32,2,64,128]{3,2,1,0:T(8,128)}), f32[32,2,64,128]{3,2,1,0:T(8,128)S(1)}, u32[]{:S(2)}, u32[]{:S(2)}) async-start(f32[32,2,64,128]{3,2,1,0:T(8,128)} %bitcast.4), calls=%async_computation | async-start | bytes 4194304 | tf_op jit(solution)/shard_map/all_to_all | solution.py:187
  118.0 0.1 copy.7
  118.1 0.1 reshape.106.place
  118.2 51.3 %all-to-all-done = f32[32,2,64,128]{3,2,1,0:T(8,128)S(1)} async-done(((f32[32,2,64,128]{3,2,1,0:T(8,128)}), f32[32,2,64,128]{3,2,1,0:T(8,128)S(1)}, u32[]{:S(2)}, u32[]{:S(2)}) %all-to-all-start) | async-done | bytes 2097184 | tf_op jit(solution)/shard_map/all_to_all | solution.py:187
  169.4 1.7 shard_map.67
  (38 shorter events, 0.1 us)
Async XLA Ops:
  0.0 13.1 %collective-permute-start = (f32[64,768]{1,0:T(8,128)}, f32[64,768]{1,0:T(8,128)S(1)}, u32[]{:S(2)}, u32[]{:S(2)}) collective-permute-start(f32[64,768]{1,0:T(8,128)} %refs_9_.1), channel_id=1, source_target_pairs={{64,0},{96,32},{0,64},{32,96},{192,128},{224,160},{128,192},{160,2... | collective-permute-start | bytes 589832 | tf_op jit(solution)/shard_map/ppermute | solution.py:24
  3.2 18.4 %collective-permute-start.1 = (f32[64,768]{1,0:T(8,128)}, f32[64,768]{1,0:T(8,128)S(1)}, u32[]{:S(2)}, u32[]{:S(2)}) collective-permute-start(f32[64,768]{1,0:T(8,128)} %refs_9_.1), channel_id=1, source_target_pairs={{192,0},{224,32},{128,64},{160,96},{64,128},{96,160},{0,192},{32,2... | collective-permute-start | bytes 589832 | tf_op jit(solution)/shard_map/ppermute | solution.py:24
  6.0 15.6 %collective-permute-start.2 = (f32[64,768]{1,0:T(8,128)}, f32[64,768]{1,0:T(8,128)S(1)}, u32[]{:S(2)}, u32[]{:S(2)}) collective-permute-start(f32[64,768]{1,0:T(8,128)} %refs_9_.1), channel_id=1, source_target_pairs={{32,0},{64,32},{96,64},{0,96},{160,128},{192,160},{224,192},{128,2... | collective-permute-start | bytes 589832 | tf_op jit(solution)/shard_map/ppermute | solution.py:24
  9.0 12.6 %collective-permute-start.3 = (f32[64,768]{1,0:T(8,128)}, f32[64,768]{1,0:T(8,128)S(1)}, u32[]{:S(2)}, u32[]{:S(2)}) collective-permute-start(f32[64,768]{1,0:T(8,128)} %refs_9_.1), channel_id=1, source_target_pairs={{160,0},{192,32},{224,64},{128,96},{32,128},{64,160},{96,192},{0,2... | collective-permute-start | bytes 589832 | tf_op jit(solution)/shard_map/ppermute | solution.py:24
  9.7 11.9 %collective-permute-start.4 = (f32[64,768]{1,0:T(8,128)}, f32[64,768]{1,0:T(8,128)S(1)}, u32[]{:S(2)}, u32[]{:S(2)}) collective-permute-start(f32[64,768]{1,0:T(8,128)} %refs_9_.1), channel_id=1, source_target_pairs={{96,0},{0,32},{32,64},{64,96},{224,128},{128,160},{160,192},{192,2... | collective-permute-start | bytes 589832 | tf_op jit(solution)/shard_map/ppermute | solution.py:24
  13.1 15.9 %copy-start.7 = (f32[64,768]{1,0:T(8,128)}, f32[64,768]{1,0:T(8,128)S(1)}, u32[]{:S(2)}) copy-start(f32[64,768]{1,0:T(8,128)S(1)} %collective-permute-done.refs_3_) | copy-start | bytes 589828
  13.1 14.2 %collective-permute-start.5 = (f32[64,768]{1,0:T(8,128)}, f32[64,768]{1,0:T(8,128)S(1)}, u32[]{:S(2)}, u32[]{:S(2)}) collective-permute-start(f32[64,768]{1,0:T(8,128)} %refs_9_.1), channel_id=1, source_target_pairs={{224,0},{128,32},{160,64},{192,96},{96,128},{0,160},{32,192},{64,2... | collective-permute-start | bytes 589832 | tf_op jit(solution)/shard_map/ppermute | solution.py:24
  21.6 7.4 %copy-start.8 = (f32[64,768]{1,0:T(8,128)}, f32[64,768]{1,0:T(8,128)S(1)}, u32[]{:S(2)}) copy-start(f32[64,768]{1,0:T(8,128)S(1)} %collective-permute-done.1.refs_4_) | copy-start | bytes 589828
  21.6 7.4 %collective-permute-start.6 = (f32[64,768]{1,0:T(8,128)}, f32[64,768]{1,0:T(8,128)S(1)}, u32[]{:S(2)}, u32[]{:S(2)}) collective-permute-start(f32[64,768]{1,0:T(8,128)} %refs_9_.1), channel_id=1, source_target_pairs={{128,0},{160,32},{192,64},{224,96},{0,128},{32,160},{64,192},{96,2... | collective-permute-start | bytes 589832 | tf_op jit(solution)/shard_map/ppermute | solution.py:24
  21.6 7.4 %copy-start.9 = (f32[64,768]{1,0:T(8,128)}, f32[64,768]{1,0:T(8,128)S(1)}, u32[]{:S(2)}) copy-start(f32[64,768]{1,0:T(8,128)S(1)} %collective-permute-done.2.refs_5_) | copy-start | bytes 589828
  21.6 7.4 %copy-start.10 = (f32[64,768]{1,0:T(8,128)}, f32[64,768]{1,0:T(8,128)S(1)}, u32[]{:S(2)}) copy-start(f32[64,768]{1,0:T(8,128)S(1)} %collective-permute-done.3.refs_6_) | copy-start | bytes 589828
  21.6 7.4 %copy-start.11 = (f32[64,768]{1,0:T(8,128)}, f32[64,768]{1,0:T(8,128)S(1)}, u32[]{:S(2)}) copy-start(f32[64,768]{1,0:T(8,128)S(1)} %collective-permute-done.4.refs_7_) | copy-start | bytes 589828
  27.3 1.7 %copy-start.12 = (f32[64,768]{1,0:T(8,128)}, f32[64,768]{1,0:T(8,128)S(1)}, u32[]{:S(2)}) copy-start(f32[64,768]{1,0:T(8,128)S(1)} %collective-permute-done.5.refs_8_) | copy-start | bytes 589828
  29.0 0.7 copy-start.13
  29.6 18.6 %copy-start.6 = (s32[32,32]{1,0:T(8,128)S(1)}, s32[32,32]{1,0:T(8,128)}, u32[]{:S(2)}) copy-start(s32[32,32]{1,0:T(8,128)} %param.10) | copy-start | bytes 12292
  44.0 24.1 %copy-start.2 = (f32[2,16,40,128]{3,2,1,0:T(8,128)S(1)}, f32[2,16,40,128]{3,2,1,0:T(8,128)}, u32[]{:S(2)}) copy-start(f32[2,16,40,128]{3,2,1,0:T(8,128)} %get-tuple-element.20) | copy-start | bytes 1966084
  44.0 45.6 %collective-permute-start.14 = (f32[4,32,24,128]{3,2,1,0:T(8,128)}, f32[4,32,24,128]{3,2,1,0:T(8,128)S(1)}, u32[]{:S(2)}, u32[]{:S(2)}) collective-permute-start(f32[4,32,24,128]{3,2,1,0:T(8,128)} %get-tuple-element.29), channel_id=1, source_target_pairs={{128,0},{160,32},{192,64},{224,96},{0,128},{32,160},{64,192},{96,2... | collective-permute-start | bytes 4718600 | tf_op jit(solution)/shard_map/ppermute | solution.py:24
  46.2 17.9 %collective-permute-start.11 = (f32[2,16,40,128]{3,2,1,0:T(8,128)}, f32[2,16,40,128]{3,2,1,0:T(8,128)S(1)}, u32[]{:S(2)}, u32[]{:S(2)}) collective-permute-start(f32[2,16,40,128]{3,2,1,0:T(8,128)} %get-tuple-element.25), channel_id=1, source_target_pairs={{32,0},{64,32},{96,64},{0,96},{160,128},{192,160},{224,192},{128,2... | collective-permute-start | bytes 1966088 | tf_op jit(solution)/shard_map/ppermute | solution.py:24
  47.4 20.6 %collective-permute-start.7 = (f32[2,16,40,128]{3,2,1,0:T(8,128)}, f32[2,16,40,128]{3,2,1,0:T(8,128)S(1)}, u32[]{:S(2)}, u32[]{:S(2)}) collective-permute-start(f32[2,16,40,128]{3,2,1,0:T(8,128)} %get-tuple-element.21), channel_id=1, source_target_pairs={{96,0},{0,32},{32,64},{64,96},{224,128},{128,160},{160,192},{192,2... | collective-permute-start | bytes 1966088 | tf_op jit(solution)/shard_map/ppermute | solution.py:24
  49.7 27.3 %collective-permute-start.10 = (f32[2,16,40,128]{3,2,1,0:T(8,128)}, f32[2,16,40,128]{3,2,1,0:T(8,128)S(1)}, u32[]{:S(2)}, u32[]{:S(2)}) collective-permute-start(f32[2,16,40,128]{3,2,1,0:T(8,128)} %get-tuple-element.23), channel_id=1, source_target_pairs={{32,0},{64,32},{96,64},{0,96},{160,128},{192,160},{224,192},{128,2... | collective-permute-start | bytes 1966088 | tf_op jit(solution)/shard_map/ppermute | solution.py:24
  52.2 28.3 %collective-permute-start.9 = (f32[2,16,40,128]{3,2,1,0:T(8,128)}, f32[2,16,40,128]{3,2,1,0:T(8,128)S(1)}, u32[]{:S(2)}, u32[]{:S(2)}) collective-permute-start(f32[2,16,40,128]{3,2,1,0:T(8,128)} %get-tuple-element.22), channel_id=1, source_target_pairs={{96,0},{0,32},{32,64},{64,96},{224,128},{128,160},{160,192},{192,2... | collective-permute-start | bytes 1966088 | tf_op jit(solution)/shard_map/ppermute | solution.py:24
  64.1 23.9 %copy-start = (f32[2,32,40,128]{3,2,1,0:T(8,128)S(1)}, f32[2,32,40,128]{3,2,1,0:T(8,128)}, u32[]{:S(2)}) copy-start(f32[2,32,40,128]{3,2,1,0:T(8,128)} %get-tuple-element.19.own) | copy-start | bytes 3932164
  65.3 19.2 %collective-permute-start.12 = (f32[2,16,40,128]{3,2,1,0:T(8,128)S(1)}, f32[2,16,40,128]{3,2,1,0:T(8,128)S(1)}, u32[]{:S(2)}, u32[]{:S(2)}) collective-permute-start(f32[2,16,40,128]{3,2,1,0:T(8,128)S(1)} %add.41), channel_id=1, source_target_pairs={{32,0},{64,32},{96,64},{0,96},{160,128},{192,160},{224,192},{128,2... | collective-permute-start | bytes 1966088 | tf_op jit(solution)/shard_map/ppermute | solution.py:24
  68.1 19.8 %collective-permute-start.8 = (f32[2,16,40,128]{3,2,1,0:T(8,128)S(1)}, f32[2,16,40,128]{3,2,1,0:T(8,128)S(1)}, u32[]{:S(2)}, u32[]{:S(2)}) collective-permute-start(f32[2,16,40,128]{3,2,1,0:T(8,128)S(1)} %add.40), channel_id=1, source_target_pairs={{96,0},{0,32},{32,64},{64,96},{224,128},{128,160},{160,192},{192,2... | collective-permute-start | bytes 1966088 | tf_op jit(solution)/shard_map/ppermute | solution.py:24
  87.9 1.7 copy-start.3
  87.9 1.7 copy-start.4
  87.9 1.7 copy-start.5
  89.0 12.3 %collective-permute-start.13 = (f32[32,40,128]{2,1,0:T(8,128)}, f32[32,40,128]{2,1,0:T(8,128)S(1)}, u32[]{:S(2)}, u32[]{:S(2)}) collective-permute-start(f32[32,40,128]{2,1,0:T(8,128)} %get-tuple-element.27), channel_id=1, source_target_pairs={{128,0},{160,32},{192,64},{224,96},{0,128},{32,160},{64,192},{96,2... | collective-permute-start | bytes 1966088 | tf_op jit(solution)/shard_map/ppermute | solution.py:24
  89.6 15.2 %copy-start.1 = (f32[32,24,128]{2,1,0:T(8,128)S(1)}, f32[32,24,128]{2,1,0:T(8,128)}, u32[]{:S(2)}) copy-start(f32[32,24,128]{2,1,0:T(8,128)} %get-tuple-element.28.own) | copy-start | bytes 1179652
  90.7 10.5 %collective-permute-start.15 = (f32[32,24,128]{2,1,0:T(8,128)}, f32[32,24,128]{2,1,0:T(8,128)}, u32[]{:S(2)}, u32[]{:S(2)}) collective-permute-start(f32[32,24,128]{2,1,0:T(8,128)} %get-tuple-element.37), channel_id=1, source_target_pairs={{64,0},{96,32},{0,64},{32,96},{192,128},{224,160},{128,192},{160,2... | collective-permute-start | bytes 1179656 | tf_op jit(solution)/shard_map/ppermute | solution.py:24
  90.7 14.2 %collective-permute-start.16 = (f32[32,24,128]{2,1,0:T(8,128)}, f32[32,24,128]{2,1,0:T(8,128)}, u32[]{:S(2)}, u32[]{:S(2)}) collective-permute-start(f32[32,24,128]{2,1,0:T(8,128)} %get-tuple-element.36), channel_id=1, source_target_pairs={{96,0},{0,32},{32,64},{64,96},{224,128},{128,160},{160,192},{192,2... | collective-permute-start | bytes 1179656 | tf_op jit(solution)/shard_map/ppermute | solution.py:24
  91.9 13.0 %collective-permute-start.17 = (f32[32,24,128]{2,1,0:T(8,128)}, f32[32,24,128]{2,1,0:T(8,128)}, u32[]{:S(2)}, u32[]{:S(2)}) collective-permute-start(f32[32,24,128]{2,1,0:T(8,128)} %get-tuple-element.35), channel_id=1, source_target_pairs={{32,0},{64,32},{96,64},{0,96},{160,128},{192,160},{224,192},{128,2... | collective-permute-start | bytes 1179656 | tf_op jit(solution)/shard_map/ppermute | solution.py:24
  107.9 61.5 %all-to-all-start = ((f32[32,2,64,128]{3,2,1,0:T(8,128)}), f32[32,2,64,128]{3,2,1,0:T(8,128)S(1)}, u32[]{:S(2)}, u32[]{:S(2)}) async-start(f32[32,2,64,128]{3,2,1,0:T(8,128)} %bitcast.4), calls=%async_computation | async-start | bytes 4194304 | tf_op jit(solution)/shard_map/all_to_all | solution.py:187

commit v3 on v2

--- a/solution.py
+++ b/solution.py
@@ -88,7 +88,7 @@
             high = a.astype(jnp.bfloat16)
             x_ref[c, here, :width] = high
             x_ref[c, here, width:] = (a - high.astype(jnp.float32)).astype(jnp.bfloat16)
-    step = 4
+    step = 8
 
     def body(k, carry):
         results = []

time: 171 us -> 170 us (level)
  no operation moved by 1% of the time
where the time goes in v3:
time: 170 us
  waiting for transfers between devices  101 us (59%)
  starting transfers between devices  43 us (25%)
  Pallas kernels  18.6 us (11%)
  other arithmetic  5.31 us (3%)
    all_to_all x1, waiting for transfers between devices, to_owners(): lax.all_to_all(padded.reshape(groups, n // groups, rows, width), 'vir', 0...  51.3 us
    ppermute x18, waiting for transfers between devices, from_occ(): return lax.ppermute(v, 'occ', perm)  50.2 us
    ppermute x18, starting transfers between devices, from_occ(): return lax.ppermute(v, 'occ', perm)  33 us
    pallas_call x1, Pallas kernels, products(): call(functools.partial(product_kernel, len(pieces), moves), shapes, [smem...  12.9 us
    all_to_all x1, starting transfers between devices, to_owners(): lax.all_to_all(padded.reshape(groups, n // groups, rows, width), 'vir', 0...  10.1 us
  transfers between devices with their start and end apart: 19, of which 11 were waited for; matrix products, arithmetic and copies ran while one was open for 3% of the time, Pallas kernels for 1%

profile of v3, /device:TPU:32, one launch (start us, length us, event | category | flops | bytes accessed | tf_op | source)
XLA Modules:
  0.0 169.7 jit_solution(17972562693972309451)
XLA Ops:
  0.0 3.2 %collective-permute-start = (f32[64,768]{1,0:T(8,128)}, f32[64,768]{1,0:T(8,128)S(1)}, u32[]{:S(2)}, u32[]{:S(2)}) collective-permute-start(f32[64,768]{1,0:T(8,128)} %refs_9_.1), channel_id=1, source_target_pairs={{64,0},{96,32},{0,64},{32,96},{192,128},{224,160},{128,192},{160,2... | collective-permute-start | bytes 589832 | tf_op jit(solution)/shard_map/ppermute | solution.py:24
  3.2 2.8 %collective-permute-start.1 = (f32[64,768]{1,0:T(8,128)}, f32[64,768]{1,0:T(8,128)S(1)}, u32[]{:S(2)}, u32[]{:S(2)}) collective-permute-start(f32[64,768]{1,0:T(8,128)} %refs_9_.1), channel_id=1, source_target_pairs={{192,0},{224,32},{128,64},{160,96},{64,128},{96,160},{0,192},{32,2... | collective-permute-start | bytes 589832 | tf_op jit(solution)/shard_map/ppermute | solution.py:24
  6.0 3.0 %collective-permute-start.2 = (f32[64,768]{1,0:T(8,128)}, f32[64,768]{1,0:T(8,128)S(1)}, u32[]{:S(2)}, u32[]{:S(2)}) collective-permute-start(f32[64,768]{1,0:T(8,128)} %refs_9_.1), channel_id=1, source_target_pairs={{32,0},{64,32},{96,64},{0,96},{160,128},{192,160},{224,192},{128,2... | collective-permute-start | bytes 589832 | tf_op jit(solution)/shard_map/ppermute | solution.py:24
  9.0 0.7 collective-permute-start.3
  9.7 1.3 collective-permute-start.4
  11.0 2.1 %collective-permute-done.refs_3_ = f32[64,768]{1,0:T(8,128)S(1)} collective-permute-done((f32[64,768]{1,0:T(8,128)}, f32[64,768]{1,0:T(8,128)S(1)}, u32[]{:S(2)}, u32[]{:S(2)}) %collective-permute-start) | collective-permute-done | bytes 196640 | tf_op jit(solution)/shard_map/ppermute | solution.py:24
  13.1 8.5 %collective-permute-start.5 = (f32[64,768]{1,0:T(8,128)}, f32[64,768]{1,0:T(8,128)S(1)}, u32[]{:S(2)}, u32[]{:S(2)}) collective-permute-start(f32[64,768]{1,0:T(8,128)} %refs_9_.1), channel_id=1, source_target_pairs={{224,0},{128,32},{160,64},{192,96},{96,128},{0,160},{32,192},{64,2... | collective-permute-start | bytes 589832 | tf_op jit(solution)/shard_map/ppermute | solution.py:24
  21.6 0.0 collective-permute-done.1.refs_4_
  21.6 0.0 collective-permute-start.6
  21.6 0.0 collective-permute-done.2.refs_5_
  21.6 0.0 collective-permute-done.3.refs_6_
  21.6 5.6 %collective-permute-done.5.refs_8_ = f32[64,768]{1,0:T(8,128)S(1)} collective-permute-done((f32[64,768]{1,0:T(8,128)}, f32[64,768]{1,0:T(8,128)S(1)}, u32[]{:S(2)}, u32[]{:S(2)}) %collective-permute-start.5) | collective-permute-done | bytes 196640 | tf_op jit(solution)/shard_map/ppermute | solution.py:24
  27.3 1.7 collective-permute-done.6.refs_10_
  29.0 0.6 copy-done.13
  29.6 12.9 %shard_map.64 = (f32[2,16,40,128]{3,2,1,0:T(8,128)}, f32[2,16,40,128]{3,2,1,0:T(8,128)}, f32[2,16,40,128]{3,2,1,0:T(8,128)}, f32[2,16,40,128]{3,2,1,0:T(8,128)},...) custom-call(s32[1,64]{1,0:T(1,128)} %refs_0_.1, ...), custom_call_target="tpu_custom_call" | custom-call | flops 4294967296 | bytes 14155776 | tf_op jit(solution)/shard_map/pallas_call | solution.py:128
  42.6 2.2 %collective-permute-start.14 = (f32[4,32,24,128]{3,2,1,0:T(8,128)}, f32[4,32,24,128]{3,2,1,0:T(8,128)S(1)}, u32[]{:S(2)}, u32[]{:S(2)}) collective-permute-start(f32[4,32,24,128]{3,2,1,0:T(8,128)} %get-tuple-element.29), channel_id=1, source_target_pairs={{128,0},{160,32},{192,64},{224,96},{0,128},{32,160},{64,192},{96,2... | collective-permute-start | bytes 4718600 | tf_op jit(solution)/shard_map/ppermute | solution.py:24
  44.7 1.3 collective-permute-start.11
  46.0 0.8 collective-permute-start.7
  46.8 1.5 select_reduce_fusion
  48.2 2.7 %collective-permute-start.10 = (f32[2,16,40,128]{3,2,1,0:T(8,128)}, f32[2,16,40,128]{3,2,1,0:T(8,128)S(1)}, u32[]{:S(2)}, u32[]{:S(2)}) collective-permute-start(f32[2,16,40,128]{3,2,1,0:T(8,128)} %get-tuple-element.23), channel_id=1, source_target_pairs={{32,0},{64,32},{96,64},{0,96},{160,128},{192,160},{224,192},{128,2... | collective-permute-start | bytes 1966088 | tf_op jit(solution)/shard_map/ppermute | solution.py:24
  51.0 11.6 %collective-permute-done.11 = f32[2,16,40,128]{3,2,1,0:T(8,128)S(1)} collective-permute-done((f32[2,16,40,128]{3,2,1,0:T(8,128)}, f32[2,16,40,128]{3,2,1,0:T(8,128)S(1)}, u32[]{:S(2)}, u32[]{:S(2)}) %collective-permute-start.11) | collective-permute-done | bytes 655392 | tf_op jit(solution)/shard_map/ppermute | solution.py:24
  62.6 1.3 add.41
  63.9 2.6 %collective-permute-start.12 = (f32[2,16,40,128]{3,2,1,0:T(8,128)S(1)}, f32[2,16,40,128]{3,2,1,0:T(8,128)S(1)}, u32[]{:S(2)}, u32[]{:S(2)}) collective-permute-start(f32[2,16,40,128]{3,2,1,0:T(8,128)S(1)} %add.41), channel_id=1, source_target_pairs={{32,0},{64,32},{96,64},{0,96},{160,128},{192,160},{224,192},{128,2... | collective-permute-start | bytes 1966088 | tf_op jit(solution)/shard_map/ppermute | solution.py:24
  66.4 0.1 add.40
  66.5 0.1 collective-permute-start.8
  66.6 0.1 select_reduce_fusion.3
  66.7 8.8 %collective-permute-done.10.right_a = f32[2,16,40,128]{3,2,1,0:T(8,128)S(1)} collective-permute-done((f32[2,16,40,128]{3,2,1,0:T(8,128)}, f32[2,16,40,128]{3,2,1,0:T(8,128)S(1)}, u32[]{:S(2)}, u32[]{:S(2)}) %collective-permute-start.10) | collective-permute-done | bytes 655392 | tf_op jit(solution)/shard_map/ppermute | solution.py:24
  75.6 3.6 %collective-permute-done.9.left_b = f32[2,16,40,128]{3,2,1,0:T(8,128)S(1)} collective-permute-done((f32[2,16,40,128]{3,2,1,0:T(8,128)}, f32[2,16,40,128]{3,2,1,0:T(8,128)S(1)}, u32[]{:S(2)}, u32[]{:S(2)}) %collective-permute-start.9) | collective-permute-done | bytes 655392 | tf_op jit(solution)/shard_map/ppermute | solution.py:24
  79.1 3.9 %collective-permute-done.12.right_b = f32[2,16,40,128]{3,2,1,0:T(8,128)S(1)} collective-permute-done((f32[2,16,40,128]{3,2,1,0:T(8,128)S(1)}, f32[2,16,40,128]{3,2,1,0:T(8,128)S(1)}, u32[]{:S(2)}, u32[]{:S(2)}) %collective-permute-start.12) | collective-permute-done | bytes 655392 | tf_op jit(solution)/shard_map/ppermute | solution.py:24
  83.1 3.4 %collective-permute-done.8.left_a = f32[2,16,40,128]{3,2,1,0:T(8,128)S(1)} collective-permute-done((f32[2,16,40,128]{3,2,1,0:T(8,128)S(1)}, f32[2,16,40,128]{3,2,1,0:T(8,128)S(1)}, u32[]{:S(2)}, u32[]{:S(2)}) %collective-permute-start.8) | collective-permute-done | bytes 655392 | tf_op jit(solution)/shard_map/ppermute | solution.py:24
  86.5 1.0 shard_map.65
  87.5 0.7 collective-permute-start.13
  88.2 1.1 fusion
  89.3 1.2 collective-permute-start.16
  90.4 2.1 %collective-permute-start.17 = (f32[32,24,128]{2,1,0:T(8,128)}, f32[32,24,128]{2,1,0:T(8,128)}, u32[]{:S(2)}, u32[]{:S(2)}) collective-permute-start(f32[32,24,128]{2,1,0:T(8,128)} %get-tuple-element.35), channel_id=1, source_target_pairs={{32,0},{64,32},{96,64},{0,96},{160,128},{192,160},{224,192},{128,2... | collective-permute-start | bytes 1179656 | tf_op jit(solution)/shard_map/ppermute | solution.py:24
  92.5 1.2 convert_reduce_fusion
  93.7 0.2 select_reduce_fusion.1
  93.9 0.1 copy.8
  93.9 0.1 reshape.107.table
  94.0 5.8 %collective-permute-done.13.other_a = f32[32,40,128]{2,1,0:T(8,128)S(1)} collective-permute-done((f32[32,40,128]{2,1,0:T(8,128)}, f32[32,40,128]{2,1,0:T(8,128)S(1)}, u32[]{:S(2)}, u32[]{:S(2)}) %collective-permute-start.13) | collective-permute-done | bytes 655392 | tf_op jit(solution)/shard_map/ppermute | solution.py:24
  99.8 0.0 collective-permute-done.15.far
  99.8 3.6 %collective-permute-done.16.up = f32[32,24,128]{2,1,0:T(8,128)} collective-permute-done((f32[32,24,128]{2,1,0:T(8,128)}, f32[32,24,128]{2,1,0:T(8,128)}, u32[]{:S(2)}, u32[]{:S(2)}) %collective-permute-start.16) | collective-permute-done | bytes 393248 | tf_op jit(solution)/shard_map/ppermute | solution.py:24
  103.4 3.0 %shard_map.66 = f32[64,64,128]{2,1,0:T(8,128)} custom-call(s32[64]{0:T(128)S(1)} %reshape.107.table, f32[32,40,128]{2,1,0:T(8,128)S(1)} %get-tuple-element.26.keep, f32[32,40,128]{2,1,0:T(8,128)S(1)} %collective-permute-done.13.other_a, f32[32,24,128]{2,1,0:T(8,128)S(1)} %copy-done.1, f32[4,32,24,128]{3,2,1,0:T(8,128)S(1)} %collective-permute-done.14.other_b, ...), custom_call_target="tpu_custom_call" | custom-call | bytes 6291456 | tf_op jit(solution)/shard_map/pallas_call | solution.py:180
  106.5 10.1 %all-to-all-start = ((f32[32,2,64,128]{3,2,1,0:T(8,128)}), f32[32,2,64,128]{3,2,1,0:T(8,128)S(1)}, u32[]{:S(2)}, u32[]{:S(2)}) async-start(f32[32,2,64,128]{3,2,1,0:T(8,128)} %bitcast.4), calls=%async_computation | async-start | bytes 4194304 | tf_op jit(solution)/shard_map/all_to_all | solution.py:187
  116.5 0.1 copy.7
  116.6 0.1 reshape.106.place
  116.7 51.3 %all-to-all-done = f32[32,2,64,128]{3,2,1,0:T(8,128)S(1)} async-done(((f32[32,2,64,128]{3,2,1,0:T(8,128)}), f32[32,2,64,128]{3,2,1,0:T(8,128)S(1)}, u32[]{:S(2)}, u32[]{:S(2)}) %all-to-all-start) | async-done | bytes 2097184 | tf_op jit(solution)/shard_map/all_to_all | solution.py:187
  168.0 1.7 shard_map.67
  (38 shorter events, 0.1 us)
Async XLA Ops:
  0.0 13.1 %collective-permute-start = (f32[64,768]{1,0:T(8,128)}, f32[64,768]{1,0:T(8,128)S(1)}, u32[]{:S(2)}, u32[]{:S(2)}) collective-permute-start(f32[64,768]{1,0:T(8,128)} %refs_9_.1), channel_id=1, source_target_pairs={{64,0},{96,32},{0,64},{32,96},{192,128},{224,160},{128,192},{160,2... | collective-permute-start | bytes 589832 | tf_op jit(solution)/shard_map/ppermute | solution.py:24
  3.2 18.4 %collective-permute-start.1 = (f32[64,768]{1,0:T(8,128)}, f32[64,768]{1,0:T(8,128)S(1)}, u32[]{:S(2)}, u32[]{:S(2)}) collective-permute-start(f32[64,768]{1,0:T(8,128)} %refs_9_.1), channel_id=1, source_target_pairs={{192,0},{224,32},{128,64},{160,96},{64,128},{96,160},{0,192},{32,2... | collective-permute-start | bytes 589832 | tf_op jit(solution)/shard_map/ppermute | solution.py:24
  6.0 15.6 %collective-permute-start.2 = (f32[64,768]{1,0:T(8,128)}, f32[64,768]{1,0:T(8,128)S(1)}, u32[]{:S(2)}, u32[]{:S(2)}) collective-permute-start(f32[64,768]{1,0:T(8,128)} %refs_9_.1), channel_id=1, source_target_pairs={{32,0},{64,32},{96,64},{0,96},{160,128},{192,160},{224,192},{128,2... | collective-permute-start | bytes 589832 | tf_op jit(solution)/shard_map/ppermute | solution.py:24
  9.0 12.6 %collective-permute-start.3 = (f32[64,768]{1,0:T(8,128)}, f32[64,768]{1,0:T(8,128)S(1)}, u32[]{:S(2)}, u32[]{:S(2)}) collective-permute-start(f32[64,768]{1,0:T(8,128)} %refs_9_.1), channel_id=1, source_target_pairs={{160,0},{192,32},{224,64},{128,96},{32,128},{64,160},{96,192},{0,2... | collective-permute-start | bytes 589832 | tf_op jit(solution)/shard_map/ppermute | solution.py:24
  9.7 11.9 %collective-permute-start.4 = (f32[64,768]{1,0:T(8,128)}, f32[64,768]{1,0:T(8,128)S(1)}, u32[]{:S(2)}, u32[]{:S(2)}) collective-permute-start(f32[64,768]{1,0:T(8,128)} %refs_9_.1), channel_id=1, source_target_pairs={{96,0},{0,32},{32,64},{64,96},{224,128},{128,160},{160,192},{192,2... | collective-permute-start | bytes 589832 | tf_op jit(solution)/shard_map/ppermute | solution.py:24
  13.1 15.9 %copy-start.7 = (f32[64,768]{1,0:T(8,128)}, f32[64,768]{1,0:T(8,128)S(1)}, u32[]{:S(2)}) copy-start(f32[64,768]{1,0:T(8,128)S(1)} %collective-permute-done.refs_3_) | copy-start | bytes 589828
  13.1 14.2 %collective-permute-start.5 = (f32[64,768]{1,0:T(8,128)}, f32[64,768]{1,0:T(8,128)S(1)}, u32[]{:S(2)}, u32[]{:S(2)}) collective-permute-start(f32[64,768]{1,0:T(8,128)} %refs_9_.1), channel_id=1, source_target_pairs={{224,0},{128,32},{160,64},{192,96},{96,128},{0,160},{32,192},{64,2... | collective-permute-start | bytes 589832 | tf_op jit(solution)/shard_map/ppermute | solution.py:24
  21.6 7.4 %copy-start.8 = (f32[64,768]{1,0:T(8,128)}, f32[64,768]{1,0:T(8,128)S(1)}, u32[]{:S(2)}) copy-start(f32[64,768]{1,0:T(8,128)S(1)} %collective-permute-done.1.refs_4_) | copy-start | bytes 589828
  21.6 7.4 %collective-permute-start.6 = (f32[64,768]{1,0:T(8,128)}, f32[64,768]{1,0:T(8,128)S(1)}, u32[]{:S(2)}, u32[]{:S(2)}) collective-permute-start(f32[64,768]{1,0:T(8,128)} %refs_9_.1), channel_id=1, source_target_pairs={{128,0},{160,32},{192,64},{224,96},{0,128},{32,160},{64,192},{96,2... | collective-permute-start | bytes 589832 | tf_op jit(solution)/shard_map/ppermute | solution.py:24
  21.6 7.4 %copy-start.9 = (f32[64,768]{1,0:T(8,128)}, f32[64,768]{1,0:T(8,128)S(1)}, u32[]{:S(2)}) copy-start(f32[64,768]{1,0:T(8,128)S(1)} %collective-permute-done.2.refs_5_) | copy-start | bytes 589828
  21.6 7.4 %copy-start.10 = (f32[64,768]{1,0:T(8,128)}, f32[64,768]{1,0:T(8,128)S(1)}, u32[]{:S(2)}) copy-start(f32[64,768]{1,0:T(8,128)S(1)} %collective-permute-done.3.refs_6_) | copy-start | bytes 589828
  21.6 7.4 %copy-start.11 = (f32[64,768]{1,0:T(8,128)}, f32[64,768]{1,0:T(8,128)S(1)}, u32[]{:S(2)}) copy-start(f32[64,768]{1,0:T(8,128)S(1)} %collective-permute-done.4.refs_7_) | copy-start | bytes 589828
  27.3 1.7 %copy-start.12 = (f32[64,768]{1,0:T(8,128)}, f32[64,768]{1,0:T(8,128)S(1)}, u32[]{:S(2)}) copy-start(f32[64,768]{1,0:T(8,128)S(1)} %collective-permute-done.5.refs_8_) | copy-start | bytes 589828
  29.0 0.7 copy-start.13
  29.6 17.1 %copy-start.6 = (s32[32,32]{1,0:T(8,128)S(1)}, s32[32,32]{1,0:T(8,128)}, u32[]{:S(2)}) copy-start(s32[32,32]{1,0:T(8,128)} %param.10) | copy-start | bytes 12292
  42.5 23.9 %copy-start.2 = (f32[2,16,40,128]{3,2,1,0:T(8,128)S(1)}, f32[2,16,40,128]{3,2,1,0:T(8,128)}, u32[]{:S(2)}) copy-start(f32[2,16,40,128]{3,2,1,0:T(8,128)} %get-tuple-element.20) | copy-start | bytes 1966084
  42.6 45.6 %collective-permute-start.14 = (f32[4,32,24,128]{3,2,1,0:T(8,128)}, f32[4,32,24,128]{3,2,1,0:T(8,128)S(1)}, u32[]{:S(2)}, u32[]{:S(2)}) collective-permute-start(f32[4,32,24,128]{3,2,1,0:T(8,128)} %get-tuple-element.29), channel_id=1, source_target_pairs={{128,0},{160,32},{192,64},{224,96},{0,128},{32,160},{64,192},{96,2... | collective-permute-start | bytes 4718600 | tf_op jit(solution)/shard_map/ppermute | solution.py:24
  44.7 17.9 %collective-permute-start.11 = (f32[2,16,40,128]{3,2,1,0:T(8,128)}, f32[2,16,40,128]{3,2,1,0:T(8,128)S(1)}, u32[]{:S(2)}, u32[]{:S(2)}) collective-permute-start(f32[2,16,40,128]{3,2,1,0:T(8,128)} %get-tuple-element.25), channel_id=1, source_target_pairs={{32,0},{64,32},{96,64},{0,96},{160,128},{192,160},{224,192},{128,2... | collective-permute-start | bytes 1966088 | tf_op jit(solution)/shard_map/ppermute | solution.py:24
  46.0 20.4 %collective-permute-start.7 = (f32[2,16,40,128]{3,2,1,0:T(8,128)}, f32[2,16,40,128]{3,2,1,0:T(8,128)S(1)}, u32[]{:S(2)}, u32[]{:S(2)}) collective-permute-start(f32[2,16,40,128]{3,2,1,0:T(8,128)} %get-tuple-element.21), channel_id=1, source_target_pairs={{96,0},{0,32},{32,64},{64,96},{224,128},{128,160},{160,192},{192,2... | collective-permute-start | bytes 1966088 | tf_op jit(solution)/shard_map/ppermute | solution.py:24
  48.2 27.3 %collective-permute-start.10 = (f32[2,16,40,128]{3,2,1,0:T(8,128)}, f32[2,16,40,128]{3,2,1,0:T(8,128)S(1)}, u32[]{:S(2)}, u32[]{:S(2)}) collective-permute-start(f32[2,16,40,128]{3,2,1,0:T(8,128)} %get-tuple-element.23), channel_id=1, source_target_pairs={{32,0},{64,32},{96,64},{0,96},{160,128},{192,160},{224,192},{128,2... | collective-permute-start | bytes 1966088 | tf_op jit(solution)/shard_map/ppermute | solution.py:24
  51.0 28.2 %collective-permute-start.9 = (f32[2,16,40,128]{3,2,1,0:T(8,128)}, f32[2,16,40,128]{3,2,1,0:T(8,128)S(1)}, u32[]{:S(2)}, u32[]{:S(2)}) collective-permute-start(f32[2,16,40,128]{3,2,1,0:T(8,128)} %get-tuple-element.22), channel_id=1, source_target_pairs={{96,0},{0,32},{32,64},{64,96},{224,128},{128,160},{160,192},{192,2... | collective-permute-start | bytes 1966088 | tf_op jit(solution)/shard_map/ppermute | solution.py:24
  62.6 23.9 %copy-start = (f32[2,32,40,128]{3,2,1,0:T(8,128)S(1)}, f32[2,32,40,128]{3,2,1,0:T(8,128)}, u32[]{:S(2)}) copy-start(f32[2,32,40,128]{3,2,1,0:T(8,128)} %get-tuple-element.19.own) | copy-start | bytes 3932164
  63.9 19.2 %collective-permute-start.12 = (f32[2,16,40,128]{3,2,1,0:T(8,128)S(1)}, f32[2,16,40,128]{3,2,1,0:T(8,128)S(1)}, u32[]{:S(2)}, u32[]{:S(2)}) collective-permute-start(f32[2,16,40,128]{3,2,1,0:T(8,128)S(1)} %add.41), channel_id=1, source_target_pairs={{32,0},{64,32},{96,64},{0,96},{160,128},{192,160},{224,192},{128,2... | collective-permute-start | bytes 1966088 | tf_op jit(solution)/shard_map/ppermute | solution.py:24
  66.5 20.0 %collective-permute-start.8 = (f32[2,16,40,128]{3,2,1,0:T(8,128)S(1)}, f32[2,16,40,128]{3,2,1,0:T(8,128)S(1)}, u32[]{:S(2)}, u32[]{:S(2)}) collective-permute-start(f32[2,16,40,128]{3,2,1,0:T(8,128)S(1)} %add.40), channel_id=1, source_target_pairs={{96,0},{0,32},{32,64},{64,96},{224,128},{128,160},{160,192},{192,2... | collective-permute-start | bytes 1966088 | tf_op jit(solution)/shard_map/ppermute | solution.py:24
  86.5 1.7 %copy-start.3 = (f32[32,24,128]{2,1,0:T(8,128)S(1)}, f32[32,24,128]{2,1,0:T(8,128)}, u32[]{:S(2)}) copy-start(f32[32,24,128]{2,1,0:T(8,128)} %get-tuple-element.30) | copy-start | bytes 1179652
  86.5 1.7 %copy-start.4 = (f32[32,24,128]{2,1,0:T(8,128)S(1)}, f32[32,24,128]{2,1,0:T(8,128)}, u32[]{:S(2)}) copy-start(f32[32,24,128]{2,1,0:T(8,128)} %get-tuple-element.31) | copy-start | bytes 1179652
  86.5 1.7 %copy-start.5 = (f32[32,24,128]{2,1,0:T(8,128)S(1)}, f32[32,24,128]{2,1,0:T(8,128)}, u32[]{:S(2)}) copy-start(f32[32,24,128]{2,1,0:T(8,128)} %get-tuple-element.32) | copy-start | bytes 1179652
  87.5 12.3 %collective-permute-start.13 = (f32[32,40,128]{2,1,0:T(8,128)}, f32[32,40,128]{2,1,0:T(8,128)S(1)}, u32[]{:S(2)}, u32[]{:S(2)}) collective-permute-start(f32[32,40,128]{2,1,0:T(8,128)} %get-tuple-element.27), channel_id=1, source_target_pairs={{128,0},{160,32},{192,64},{224,96},{0,128},{32,160},{64,192},{96,2... | collective-permute-start | bytes 1966088 | tf_op jit(solution)/shard_map/ppermute | solution.py:24
  88.2 15.2 %copy-start.1 = (f32[32,24,128]{2,1,0:T(8,128)S(1)}, f32[32,24,128]{2,1,0:T(8,128)}, u32[]{:S(2)}) copy-start(f32[32,24,128]{2,1,0:T(8,128)} %get-tuple-element.28.own) | copy-start | bytes 1179652
  89.3 10.5 %collective-permute-start.15 = (f32[32,24,128]{2,1,0:T(8,128)}, f32[32,24,128]{2,1,0:T(8,128)}, u32[]{:S(2)}, u32[]{:S(2)}) collective-permute-start(f32[32,24,128]{2,1,0:T(8,128)} %get-tuple-element.37), channel_id=1, source_target_pairs={{64,0},{96,32},{0,64},{32,96},{192,128},{224,160},{128,192},{160,2... | collective-permute-start | bytes 1179656 | tf_op jit(solution)/shard_map/ppermute | solution.py:24
  89.3 14.2 %collective-permute-start.16 = (f32[32,24,128]{2,1,0:T(8,128)}, f32[32,24,128]{2,1,0:T(8,128)}, u32[]{:S(2)}, u32[]{:S(2)}) collective-permute-start(f32[32,24,128]{2,1,0:T(8,128)} %get-tuple-element.36), channel_id=1, source_target_pairs={{96,0},{0,32},{32,64},{64,96},{224,128},{128,160},{160,192},{192,2... | collective-permute-start | bytes 1179656 | tf_op jit(solution)/shard_map/ppermute | solution.py:24
  90.4 13.0 %collective-permute-start.17 = (f32[32,24,128]{2,1,0:T(8,128)}, f32[32,24,128]{2,1,0:T(8,128)}, u32[]{:S(2)}, u32[]{:S(2)}) collective-permute-start(f32[32,24,128]{2,1,0:T(8,128)} %get-tuple-element.35), channel_id=1, source_target_pairs={{32,0},{64,32},{96,64},{0,96},{160,128},{192,160},{224,192},{128,2... | collective-permute-start | bytes 1179656 | tf_op jit(solution)/shard_map/ppermute | solution.py:24
  106.5 61.5 %all-to-all-start = ((f32[32,2,64,128]{3,2,1,0:T(8,128)}), f32[32,2,64,128]{3,2,1,0:T(8,128)S(1)}, u32[]{:S(2)}, u32[]{:S(2)}) async-start(f32[32,2,64,128]{3,2,1,0:T(8,128)} %bitcast.4), calls=%async_computation | async-start | bytes 4194304 | tf_op jit(solution)/shard_map/all_to_all | solution.py:187

commit v4 on v3

--- a/solution.py
+++ b/solution.py
@@ -88,7 +88,7 @@
             high = a.astype(jnp.bfloat16)
             x_ref[c, here, :width] = high
             x_ref[c, here, width:] = (a - high.astype(jnp.float32)).astype(jnp.bfloat16)
-    step = 8
+    step = 16
 
     def body(k, carry):
         results = []

time: 170 us -> 169 us (level)
  no operation moved by 1% of the time
where the time goes in v4:
time: 169 us
  waiting for transfers between devices  102 us (60%)
  starting transfers between devices  42.8 us (25%)
  Pallas kernels  17.9 us (11%)
  other arithmetic  5.31 us (3%)
    all_to_all x1, waiting for transfers between devices, to_owners(): lax.all_to_all(padded.reshape(groups, n // groups, rows, width), 'vir', 0...  51.3 us
    ppermute x18, waiting for transfers between devices, from_occ(): return lax.ppermute(v, 'occ', perm)  50.4 us
    ppermute x18, starting transfers between devices, from_occ(): return lax.ppermute(v, 'occ', perm)  32.8 us
    pallas_call x1, Pallas kernels, products(): call(functools.partial(product_kernel, len(pieces), moves), shapes, [smem...  12.2 us
    all_to_all x1, starting transfers between devices, to_owners(): lax.all_to_all(padded.reshape(groups, n // groups, rows, width), 'vir', 0...  10 us
  transfers between devices with their start and end apart: 19, of which 11 were waited for; matrix products, arithmetic and copies ran while one was open for 3% of the time, Pallas kernels for 1%

profile of v4, /device:TPU:32, one launch (start us, length us, event | category | flops | bytes accessed | tf_op | source)
XLA Modules:
  0.0 168.9 jit_solution(11485573210068663749)
XLA Ops:
  0.0 3.2 %collective-permute-start = (f32[64,768]{1,0:T(8,128)}, f32[64,768]{1,0:T(8,128)S(1)}, u32[]{:S(2)}, u32[]{:S(2)}) collective-permute-start(f32[64,768]{1,0:T(8,128)} %refs_9_.1), channel_id=1, source_target_pairs={{64,0},{96,32},{0,64},{32,96},{192,128},{224,160},{128,192},{160,2... | collective-permute-start | bytes 589832 | tf_op jit(solution)/shard_map/ppermute | solution.py:24
  3.2 2.8 %collective-permute-start.1 = (f32[64,768]{1,0:T(8,128)}, f32[64,768]{1,0:T(8,128)S(1)}, u32[]{:S(2)}, u32[]{:S(2)}) collective-permute-start(f32[64,768]{1,0:T(8,128)} %refs_9_.1), channel_id=1, source_target_pairs={{192,0},{224,32},{128,64},{160,96},{64,128},{96,160},{0,192},{32,2... | collective-permute-start | bytes 589832 | tf_op jit(solution)/shard_map/ppermute | solution.py:24
  6.0 3.0 %collective-permute-start.2 = (f32[64,768]{1,0:T(8,128)}, f32[64,768]{1,0:T(8,128)S(1)}, u32[]{:S(2)}, u32[]{:S(2)}) collective-permute-start(f32[64,768]{1,0:T(8,128)} %refs_9_.1), channel_id=1, source_target_pairs={{32,0},{64,32},{96,64},{0,96},{160,128},{192,160},{224,192},{128,2... | collective-permute-start | bytes 589832 | tf_op jit(solution)/shard_map/ppermute | solution.py:24
  9.0 0.7 collective-permute-start.3
  9.7 1.3 collective-permute-start.4
  11.0 2.1 %collective-permute-done.refs_3_ = f32[64,768]{1,0:T(8,128)S(1)} collective-permute-done((f32[64,768]{1,0:T(8,128)}, f32[64,768]{1,0:T(8,128)S(1)}, u32[]{:S(2)}, u32[]{:S(2)}) %collective-permute-start) | collective-permute-done | bytes 196640 | tf_op jit(solution)/shard_map/ppermute | solution.py:24
  13.1 8.5 %collective-permute-start.5 = (f32[64,768]{1,0:T(8,128)}, f32[64,768]{1,0:T(8,128)S(1)}, u32[]{:S(2)}, u32[]{:S(2)}) collective-permute-start(f32[64,768]{1,0:T(8,128)} %refs_9_.1), channel_id=1, source_target_pairs={{224,0},{128,32},{160,64},{192,96},{96,128},{0,160},{32,192},{64,2... | collective-permute-start | bytes 589832 | tf_op jit(solution)/shard_map/ppermute | solution.py:24
  21.6 0.0 collective-permute-done.1.refs_4_
  21.6 0.0 collective-permute-done.2.refs_5_
  21.6 0.0 collective-permute-done.3.refs_6_
  21.6 5.6 %collective-permute-done.5.refs_8_ = f32[64,768]{1,0:T(8,128)S(1)} collective-permute-done((f32[64,768]{1,0:T(8,128)}, f32[64,768]{1,0:T(8,128)S(1)}, u32[]{:S(2)}, u32[]{:S(2)}) %collective-permute-start.5) | collective-permute-done | bytes 196640 | tf_op jit(solution)/shard_map/ppermute | solution.py:24
  27.3 1.7 %collective-permute-done.6.refs_10_ = f32[64,768]{1,0:T(8,128)S(1)} collective-permute-done((f32[64,768]{1,0:T(8,128)}, f32[64,768]{1,0:T(8,128)S(1)}, u32[]{:S(2)}, u32[]{:S(2)}) %collective-permute-start.6) | collective-permute-done | bytes 196640 | tf_op jit(solution)/shard_map/ppermute | solution.py:24
  29.0 0.6 copy-done.13
  29.6 12.2 %shard_map.64 = (f32[2,16,40,128]{3,2,1,0:T(8,128)}, f32[2,16,40,128]{3,2,1,0:T(8,128)}, f32[2,16,40,128]{3,2,1,0:T(8,128)}, f32[2,16,40,128]{3,2,1,0:T(8,128)},...) custom-call(s32[1,64]{1,0:T(1,128)} %refs_0_.1, ...), custom_call_target="tpu_custom_call" | custom-call | flops 4294967296 | bytes 14155776 | tf_op jit(solution)/shard_map/pallas_call | solution.py:128
  41.8 2.2 %collective-permute-start.14 = (f32[4,32,24,128]{3,2,1,0:T(8,128)}, f32[4,32,24,128]{3,2,1,0:T(8,128)S(1)}, u32[]{:S(2)}, u32[]{:S(2)}) collective-permute-start(f32[4,32,24,128]{3,2,1,0:T(8,128)} %get-tuple-element.29), channel_id=1, source_target_pairs={{128,0},{160,32},{192,64},{224,96},{0,128},{32,160},{64,192},{96,2... | collective-permute-start | bytes 4718600 | tf_op jit(solution)/shard_map/ppermute | solution.py:24
  44.0 1.3 collective-permute-start.11
  45.3 0.8 collective-permute-start.7
  46.1 1.5 select_reduce_fusion
  47.5 2.5 %collective-permute-start.10 = (f32[2,16,40,128]{3,2,1,0:T(8,128)}, f32[2,16,40,128]{3,2,1,0:T(8,128)S(1)}, u32[]{:S(2)}, u32[]{:S(2)}) collective-permute-start(f32[2,16,40,128]{3,2,1,0:T(8,128)} %get-tuple-element.23), channel_id=1, source_target_pairs={{32,0},{64,32},{96,64},{0,96},{160,128},{192,160},{224,192},{128,2... | collective-permute-start | bytes 1966088 | tf_op jit(solution)/shard_map/ppermute | solution.py:24
  50.1 11.8 %collective-permute-done.11 = f32[2,16,40,128]{3,2,1,0:T(8,128)S(1)} collective-permute-done((f32[2,16,40,128]{3,2,1,0:T(8,128)}, f32[2,16,40,128]{3,2,1,0:T(8,128)S(1)}, u32[]{:S(2)}, u32[]{:S(2)}) %collective-permute-start.11) | collective-permute-done | bytes 655392 | tf_op jit(solution)/shard_map/ppermute | solution.py:24
  61.9 1.3 add.41
  63.2 2.5 %collective-permute-start.12 = (f32[2,16,40,128]{3,2,1,0:T(8,128)S(1)}, f32[2,16,40,128]{3,2,1,0:T(8,128)S(1)}, u32[]{:S(2)}, u32[]{:S(2)}) collective-permute-start(f32[2,16,40,128]{3,2,1,0:T(8,128)S(1)} %add.41), channel_id=1, source_target_pairs={{32,0},{64,32},{96,64},{0,96},{160,128},{192,160},{224,192},{128,2... | collective-permute-start | bytes 1966088 | tf_op jit(solution)/shard_map/ppermute | solution.py:24
  65.7 0.0 collective-permute-done.7
  65.7 0.1 add.40
  65.8 0.1 collective-permute-start.8
  65.9 0.1 select_reduce_fusion.3
  66.0 8.8 %collective-permute-done.10.right_a = f32[2,16,40,128]{3,2,1,0:T(8,128)S(1)} collective-permute-done((f32[2,16,40,128]{3,2,1,0:T(8,128)}, f32[2,16,40,128]{3,2,1,0:T(8,128)S(1)}, u32[]{:S(2)}, u32[]{:S(2)}) %collective-permute-start.10) | collective-permute-done | bytes 655392 | tf_op jit(solution)/shard_map/ppermute | solution.py:24
  74.8 3.6 %collective-permute-done.9.left_b = f32[2,16,40,128]{3,2,1,0:T(8,128)S(1)} collective-permute-done((f32[2,16,40,128]{3,2,1,0:T(8,128)}, f32[2,16,40,128]{3,2,1,0:T(8,128)S(1)}, u32[]{:S(2)}, u32[]{:S(2)}) %collective-permute-start.9) | collective-permute-done | bytes 655392 | tf_op jit(solution)/shard_map/ppermute | solution.py:24
  78.4 3.9 %collective-permute-done.12.right_b = f32[2,16,40,128]{3,2,1,0:T(8,128)S(1)} collective-permute-done((f32[2,16,40,128]{3,2,1,0:T(8,128)S(1)}, f32[2,16,40,128]{3,2,1,0:T(8,128)S(1)}, u32[]{:S(2)}, u32[]{:S(2)}) %collective-permute-start.12) | collective-permute-done | bytes 655392 | tf_op jit(solution)/shard_map/ppermute | solution.py:24
  82.3 3.4 %collective-permute-done.8.left_a = f32[2,16,40,128]{3,2,1,0:T(8,128)S(1)} collective-permute-done((f32[2,16,40,128]{3,2,1,0:T(8,128)S(1)}, f32[2,16,40,128]{3,2,1,0:T(8,128)S(1)}, u32[]{:S(2)}, u32[]{:S(2)}) %collective-permute-start.8) | collective-permute-done | bytes 655392 | tf_op jit(solution)/shard_map/ppermute | solution.py:24
  85.8 1.0 shard_map.65
  86.8 0.7 collective-permute-start.13
  87.5 1.1 fusion
  88.6 1.2 collective-permute-start.16
  89.7 2.1 %collective-permute-start.17 = (f32[32,24,128]{2,1,0:T(8,128)}, f32[32,24,128]{2,1,0:T(8,128)}, u32[]{:S(2)}, u32[]{:S(2)}) collective-permute-start(f32[32,24,128]{2,1,0:T(8,128)} %get-tuple-element.35), channel_id=1, source_target_pairs={{32,0},{64,32},{96,64},{0,96},{160,128},{192,160},{224,192},{128,2... | collective-permute-start | bytes 1179656 | tf_op jit(solution)/shard_map/ppermute | solution.py:24
  91.8 1.2 convert_reduce_fusion
  93.0 0.2 select_reduce_fusion.1
  93.1 0.1 copy.8
  93.2 0.1 reshape.107.table
  93.3 5.8 %collective-permute-done.13.other_a = f32[32,40,128]{2,1,0:T(8,128)S(1)} collective-permute-done((f32[32,40,128]{2,1,0:T(8,128)}, f32[32,40,128]{2,1,0:T(8,128)S(1)}, u32[]{:S(2)}, u32[]{:S(2)}) %collective-permute-start.13) | collective-permute-done | bytes 655392 | tf_op jit(solution)/shard_map/ppermute | solution.py:24
  99.1 0.0 collective-permute-done.15.far
  99.1 3.6 %collective-permute-done.16.up = f32[32,24,128]{2,1,0:T(8,128)} collective-permute-done((f32[32,24,128]{2,1,0:T(8,128)}, f32[32,24,128]{2,1,0:T(8,128)}, u32[]{:S(2)}, u32[]{:S(2)}) %collective-permute-start.16) | collective-permute-done | bytes 393248 | tf_op jit(solution)/shard_map/ppermute | solution.py:24
  102.7 3.0 %shard_map.66 = f32[64,64,128]{2,1,0:T(8,128)} custom-call(s32[64]{0:T(128)S(1)} %reshape.107.table, f32[32,40,128]{2,1,0:T(8,128)S(1)} %get-tuple-element.26.keep, f32[32,40,128]{2,1,0:T(8,128)S(1)} %collective-permute-done.13.other_a, f32[32,24,128]{2,1,0:T(8,128)S(1)} %copy-done.1, f32[4,32,24,128]{3,2,1,0:T(8,128)S(1)} %collective-permute-done.14.other_b, ...), custom_call_target="tpu_custom_call" | custom-call | bytes 6291456 | tf_op jit(solution)/shard_map/pallas_call | solution.py:180
  105.8 10.0 %all-to-all-start = ((f32[32,2,64,128]{3,2,1,0:T(8,128)}), f32[32,2,64,128]{3,2,1,0:T(8,128)S(1)}, u32[]{:S(2)}, u32[]{:S(2)}) async-start(f32[32,2,64,128]{3,2,1,0:T(8,128)} %bitcast.4), calls=%async_computation | async-start | bytes 4194304 | tf_op jit(solution)/shard_map/all_to_all | solution.py:187
  115.8 0.1 copy.7
  115.9 0.1 reshape.106.place
  116.0 51.3 %all-to-all-done = f32[32,2,64,128]{3,2,1,0:T(8,128)S(1)} async-done(((f32[32,2,64,128]{3,2,1,0:T(8,128)}), f32[32,2,64,128]{3,2,1,0:T(8,128)S(1)}, u32[]{:S(2)}, u32[]{:S(2)}) %all-to-all-start) | async-done | bytes 2097184 | tf_op jit(solution)/shard_map/all_to_all | solution.py:187
  167.3 1.7 shard_map.67
  (38 shorter events, 0.1 us)
Async XLA Ops:
  0.0 13.1 %collective-permute-start = (f32[64,768]{1,0:T(8,128)}, f32[64,768]{1,0:T(8,128)S(1)}, u32[]{:S(2)}, u32[]{:S(2)}) collective-permute-start(f32[64,768]{1,0:T(8,128)} %refs_9_.1), channel_id=1, source_target_pairs={{64,0},{96,32},{0,64},{32,96},{192,128},{224,160},{128,192},{160,2... | collective-permute-start | bytes 589832 | tf_op jit(solution)/shard_map/ppermute | solution.py:24
  3.2 18.4 %collective-permute-start.1 = (f32[64,768]{1,0:T(8,128)}, f32[64,768]{1,0:T(8,128)S(1)}, u32[]{:S(2)}, u32[]{:S(2)}) collective-permute-start(f32[64,768]{1,0:T(8,128)} %refs_9_.1), channel_id=1, source_target_pairs={{192,0},{224,32},{128,64},{160,96},{64,128},{96,160},{0,192},{32,2... | collective-permute-start | bytes 589832 | tf_op jit(solution)/shard_map/ppermute | solution.py:24
  6.0 15.6 %collective-permute-start.2 = (f32[64,768]{1,0:T(8,128)}, f32[64,768]{1,0:T(8,128)S(1)}, u32[]{:S(2)}, u32[]{:S(2)}) collective-permute-start(f32[64,768]{1,0:T(8,128)} %refs_9_.1), channel_id=1, source_target_pairs={{32,0},{64,32},{96,64},{0,96},{160,128},{192,160},{224,192},{128,2... | collective-permute-start | bytes 589832 | tf_op jit(solution)/shard_map/ppermute | solution.py:24
  9.0 12.6 %collective-permute-start.3 = (f32[64,768]{1,0:T(8,128)}, f32[64,768]{1,0:T(8,128)S(1)}, u32[]{:S(2)}, u32[]{:S(2)}) collective-permute-start(f32[64,768]{1,0:T(8,128)} %refs_9_.1), channel_id=1, source_target_pairs={{160,0},{192,32},{224,64},{128,96},{32,128},{64,160},{96,192},{0,2... | collective-permute-start | bytes 589832 | tf_op jit(solution)/shard_map/ppermute | solution.py:24
  9.7 11.9 %collective-permute-start.4 = (f32[64,768]{1,0:T(8,128)}, f32[64,768]{1,0:T(8,128)S(1)}, u32[]{:S(2)}, u32[]{:S(2)}) collective-permute-start(f32[64,768]{1,0:T(8,128)} %refs_9_.1), channel_id=1, source_target_pairs={{96,0},{0,32},{32,64},{64,96},{224,128},{128,160},{160,192},{192,2... | collective-permute-start | bytes 589832 | tf_op jit(solution)/shard_map/ppermute | solution.py:24
  13.1 15.9 %copy-start.7 = (f32[64,768]{1,0:T(8,128)}, f32[64,768]{1,0:T(8,128)S(1)}, u32[]{:S(2)}) copy-start(f32[64,768]{1,0:T(8,128)S(1)} %collective-permute-done.refs_3_) | copy-start | bytes 589828
  13.1 14.2 %collective-permute-start.5 = (f32[64,768]{1,0:T(8,128)}, f32[64,768]{1,0:T(8,128)S(1)}, u32[]{:S(2)}, u32[]{:S(2)}) collective-permute-start(f32[64,768]{1,0:T(8,128)} %refs_9_.1), channel_id=1, source_target_pairs={{224,0},{128,32},{160,64},{192,96},{96,128},{0,160},{32,192},{64,2... | collective-permute-start | bytes 589832 | tf_op jit(solution)/shard_map/ppermute | solution.py:24
  21.6 7.4 %copy-start.8 = (f32[64,768]{1,0:T(8,128)}, f32[64,768]{1,0:T(8,128)S(1)}, u32[]{:S(2)}) copy-start(f32[64,768]{1,0:T(8,128)S(1)} %collective-permute-done.1.refs_4_) | copy-start | bytes 589828
  21.6 7.4 %collective-permute-start.6 = (f32[64,768]{1,0:T(8,128)}, f32[64,768]{1,0:T(8,128)S(1)}, u32[]{:S(2)}, u32[]{:S(2)}) collective-permute-start(f32[64,768]{1,0:T(8,128)} %refs_9_.1), channel_id=1, source_target_pairs={{128,0},{160,32},{192,64},{224,96},{0,128},{32,160},{64,192},{96,2... | collective-permute-start | bytes 589832 | tf_op jit(solution)/shard_map/ppermute | solution.py:24
  21.6 7.4 %copy-start.9 = (f32[64,768]{1,0:T(8,128)}, f32[64,768]{1,0:T(8,128)S(1)}, u32[]{:S(2)}) copy-start(f32[64,768]{1,0:T(8,128)S(1)} %collective-permute-done.2.refs_5_) | copy-start | bytes 589828
  21.6 7.4 %copy-start.10 = (f32[64,768]{1,0:T(8,128)}, f32[64,768]{1,0:T(8,128)S(1)}, u32[]{:S(2)}) copy-start(f32[64,768]{1,0:T(8,128)S(1)} %collective-permute-done.3.refs_6_) | copy-start | bytes 589828
  21.6 7.4 %copy-start.11 = (f32[64,768]{1,0:T(8,128)}, f32[64,768]{1,0:T(8,128)S(1)}, u32[]{:S(2)}) copy-start(f32[64,768]{1,0:T(8,128)S(1)} %collective-permute-done.4.refs_7_) | copy-start | bytes 589828
  27.3 1.7 %copy-start.12 = (f32[64,768]{1,0:T(8,128)}, f32[64,768]{1,0:T(8,128)S(1)}, u32[]{:S(2)}) copy-start(f32[64,768]{1,0:T(8,128)S(1)} %collective-permute-done.5.refs_8_) | copy-start | bytes 589828
  29.0 0.7 copy-start.13
  29.6 16.4 %copy-start.6 = (s32[32,32]{1,0:T(8,128)S(1)}, s32[32,32]{1,0:T(8,128)}, u32[]{:S(2)}) copy-start(s32[32,32]{1,0:T(8,128)} %param.10) | copy-start | bytes 12292
  41.8 23.9 %copy-start.2 = (f32[2,16,40,128]{3,2,1,0:T(8,128)S(1)}, f32[2,16,40,128]{3,2,1,0:T(8,128)}, u32[]{:S(2)}) copy-start(f32[2,16,40,128]{3,2,1,0:T(8,128)} %get-tuple-element.20) | copy-start | bytes 1966084
  41.8 45.6 %collective-permute-start.14 = (f32[4,32,24,128]{3,2,1,0:T(8,128)}, f32[4,32,24,128]{3,2,1,0:T(8,128)S(1)}, u32[]{:S(2)}, u32[]{:S(2)}) collective-permute-start(f32[4,32,24,128]{3,2,1,0:T(8,128)} %get-tuple-element.29), channel_id=1, source_target_pairs={{128,0},{160,32},{192,64},{224,96},{0,128},{32,160},{64,192},{96,2... | collective-permute-start | bytes 4718600 | tf_op jit(solution)/shard_map/ppermute | solution.py:24
  44.0 17.9 %collective-permute-start.11 = (f32[2,16,40,128]{3,2,1,0:T(8,128)}, f32[2,16,40,128]{3,2,1,0:T(8,128)S(1)}, u32[]{:S(2)}, u32[]{:S(2)}) collective-permute-start(f32[2,16,40,128]{3,2,1,0:T(8,128)} %get-tuple-element.25), channel_id=1, source_target_pairs={{32,0},{64,32},{96,64},{0,96},{160,128},{192,160},{224,192},{128,2... | collective-permute-start | bytes 1966088 | tf_op jit(solution)/shard_map/ppermute | solution.py:24
  45.3 20.4 %collective-permute-start.7 = (f32[2,16,40,128]{3,2,1,0:T(8,128)}, f32[2,16,40,128]{3,2,1,0:T(8,128)S(1)}, u32[]{:S(2)}, u32[]{:S(2)}) collective-permute-start(f32[2,16,40,128]{3,2,1,0:T(8,128)} %get-tuple-element.21), channel_id=1, source_target_pairs={{96,0},{0,32},{32,64},{64,96},{224,128},{128,160},{160,192},{192,2... | collective-permute-start | bytes 1966088 | tf_op jit(solution)/shard_map/ppermute | solution.py:24
  47.5 27.3 %collective-permute-start.10 = (f32[2,16,40,128]{3,2,1,0:T(8,128)}, f32[2,16,40,128]{3,2,1,0:T(8,128)S(1)}, u32[]{:S(2)}, u32[]{:S(2)}) collective-permute-start(f32[2,16,40,128]{3,2,1,0:T(8,128)} %get-tuple-element.23), channel_id=1, source_target_pairs={{32,0},{64,32},{96,64},{0,96},{160,128},{192,160},{224,192},{128,2... | collective-permute-start | bytes 1966088 | tf_op jit(solution)/shard_map/ppermute | solution.py:24
  50.1 28.3 %collective-permute-start.9 = (f32[2,16,40,128]{3,2,1,0:T(8,128)}, f32[2,16,40,128]{3,2,1,0:T(8,128)S(1)}, u32[]{:S(2)}, u32[]{:S(2)}) collective-permute-start(f32[2,16,40,128]{3,2,1,0:T(8,128)} %get-tuple-element.22), channel_id=1, source_target_pairs={{96,0},{0,32},{32,64},{64,96},{224,128},{128,160},{160,192},{192,2... | collective-permute-start | bytes 1966088 | tf_op jit(solution)/shard_map/ppermute | solution.py:24
  61.9 23.9 %copy-start = (f32[2,32,40,128]{3,2,1,0:T(8,128)S(1)}, f32[2,32,40,128]{3,2,1,0:T(8,128)}, u32[]{:S(2)}) copy-start(f32[2,32,40,128]{3,2,1,0:T(8,128)} %get-tuple-element.19.own) | copy-start | bytes 3932164
  63.2 19.2 %collective-permute-start.12 = (f32[2,16,40,128]{3,2,1,0:T(8,128)S(1)}, f32[2,16,40,128]{3,2,1,0:T(8,128)S(1)}, u32[]{:S(2)}, u32[]{:S(2)}) collective-permute-start(f32[2,16,40,128]{3,2,1,0:T(8,128)S(1)} %add.41), channel_id=1, source_target_pairs={{32,0},{64,32},{96,64},{0,96},{160,128},{192,160},{224,192},{128,2... | collective-permute-start | bytes 1966088 | tf_op jit(solution)/shard_map/ppermute | solution.py:24
  65.8 20.0 %collective-permute-start.8 = (f32[2,16,40,128]{3,2,1,0:T(8,128)S(1)}, f32[2,16,40,128]{3,2,1,0:T(8,128)S(1)}, u32[]{:S(2)}, u32[]{:S(2)}) collective-permute-start(f32[2,16,40,128]{3,2,1,0:T(8,128)S(1)} %add.40), channel_id=1, source_target_pairs={{96,0},{0,32},{32,64},{64,96},{224,128},{128,160},{160,192},{192,2... | collective-permute-start | bytes 1966088 | tf_op jit(solution)/shard_map/ppermute | solution.py:24
  85.8 1.7 %copy-start.3 = (f32[32,24,128]{2,1,0:T(8,128)S(1)}, f32[32,24,128]{2,1,0:T(8,128)}, u32[]{:S(2)}) copy-start(f32[32,24,128]{2,1,0:T(8,128)} %get-tuple-element.30) | copy-start | bytes 1179652
  85.8 1.7 %copy-start.4 = (f32[32,24,128]{2,1,0:T(8,128)S(1)}, f32[32,24,128]{2,1,0:T(8,128)}, u32[]{:S(2)}) copy-start(f32[32,24,128]{2,1,0:T(8,128)} %get-tuple-element.31) | copy-start | bytes 1179652
  85.8 1.7 %copy-start.5 = (f32[32,24,128]{2,1,0:T(8,128)S(1)}, f32[32,24,128]{2,1,0:T(8,128)}, u32[]{:S(2)}) copy-start(f32[32,24,128]{2,1,0:T(8,128)} %get-tuple-element.32) | copy-start | bytes 1179652
  86.8 12.3 %collective-permute-start.13 = (f32[32,40,128]{2,1,0:T(8,128)}, f32[32,40,128]{2,1,0:T(8,128)S(1)}, u32[]{:S(2)}, u32[]{:S(2)}) collective-permute-start(f32[32,40,128]{2,1,0:T(8,128)} %get-tuple-element.27), channel_id=1, source_target_pairs={{128,0},{160,32},{192,64},{224,96},{0,128},{32,160},{64,192},{96,2... | collective-permute-start | bytes 1966088 | tf_op jit(solution)/shard_map/ppermute | solution.py:24
  87.5 15.2 %copy-start.1 = (f32[32,24,128]{2,1,0:T(8,128)S(1)}, f32[32,24,128]{2,1,0:T(8,128)}, u32[]{:S(2)}) copy-start(f32[32,24,128]{2,1,0:T(8,128)} %get-tuple-element.28.own) | copy-start | bytes 1179652
  88.6 10.5 %collective-permute-start.15 = (f32[32,24,128]{2,1,0:T(8,128)}, f32[32,24,128]{2,1,0:T(8,128)}, u32[]{:S(2)}, u32[]{:S(2)}) collective-permute-start(f32[32,24,128]{2,1,0:T(8,128)} %get-tuple-element.37), channel_id=1, source_target_pairs={{64,0},{96,32},{0,64},{32,96},{192,128},{224,160},{128,192},{160,2... | collective-permute-start | bytes 1179656 | tf_op jit(solution)/shard_map/ppermute | solution.py:24
  88.6 14.2 %collective-permute-start.16 = (f32[32,24,128]{2,1,0:T(8,128)}, f32[32,24,128]{2,1,0:T(8,128)}, u32[]{:S(2)}, u32[]{:S(2)}) collective-permute-start(f32[32,24,128]{2,1,0:T(8,128)} %get-tuple-element.36), channel_id=1, source_target_pairs={{96,0},{0,32},{32,64},{64,96},{224,128},{128,160},{160,192},{192,2... | collective-permute-start | bytes 1179656 | tf_op jit(solution)/shard_map/ppermute | solution.py:24
  89.7 13.0 %collective-permute-start.17 = (f32[32,24,128]{2,1,0:T(8,128)}, f32[32,24,128]{2,1,0:T(8,128)}, u32[]{:S(2)}, u32[]{:S(2)}) collective-permute-start(f32[32,24,128]{2,1,0:T(8,128)} %get-tuple-element.35), channel_id=1, source_target_pairs={{32,0},{64,32},{96,64},{0,96},{160,128},{192,160},{224,192},{128,2... | collective-permute-start | bytes 1179656 | tf_op jit(solution)/shard_map/ppermute | solution.py:24
  105.8 61.5 %all-to-all-start = ((f32[32,2,64,128]{3,2,1,0:T(8,128)}), f32[32,2,64,128]{3,2,1,0:T(8,128)S(1)}, u32[]{:S(2)}, u32[]{:S(2)}) async-start(f32[32,2,64,128]{3,2,1,0:T(8,128)} %bitcast.4), calls=%async_computation | async-start | bytes 4194304 | tf_op jit(solution)/shard_map/all_to_all | solution.py:187
